TPU v7x, 128 devices: a whole 4x4x4 slice. The times are simulated.
128 devices in a mesh: seq: 64 (over z_lo, x, y, core), dp: 2 (over z_hi).
Axes of the slice: x: 4, y: 4, z: 4 (z_hi: 2, z_lo: 2; z = z_hi * 2 + z_lo), core: 2. Of those that a mesh axis runs over, the one named last changes fastest.
Arguments:
- tokens: bfloat16 [2, 8192, 4096], P('dp', 'seq'), may hold values from -6 to 6
- queries: bfloat16 [2, 8192, 4096], P('dp', 'seq'), may hold values from -6 to 6
- keys: bfloat16 [2, 8192, 4096], P('dp', 'seq'), may hold values from -6 to 6
- values: bfloat16 [2, 8192, 4096], P('dp', 'seq'), may hold values from -6 to 6
- upstream: bfloat16 [2, 8192, 4096], P('dp', 'seq'), may hold values from -0.15625 to 0.15625
- filters: float32 [8192, 4096], P(None, 'seq'), may hold values from -4 to 4
Outputs:
- update: float32 [64, 512, 1024], P('seq', None, 'dp')
- filter_grad: float32 [8192, 4096], P('dp', 'seq')
All inputs are finite; a program needn't handle non-finite values.
Results may differ from a plain program's by a relative error of at most 0.0006.
The roundings to bfloat16 on the way count: a program that leaves them out, or rounds other values in their place, can miss the bound.
Values may be sent and summed in bfloat16 or wider, within the bound.
A program may use at most 192 MiB of HBM per device.

v0:
```python
import math

import jax
import jax.numpy as jnp
from jax import lax
from jax.sharding import PartitionSpec as P

ROW_BLOCKS = 8
NS_STEPS = 5


COEF_A = 3.4445
COEF_B = -4.775
COEF_C = 2.0315


def fourier_tables(padded_len, outer_len):
    inner_len = padded_len // outer_len
    tables_all = []
    for extent in (outer_len, inner_len):
        grid = (
            lax.broadcasted_iota(jnp.int32, (extent, extent), 0)
            * lax.broadcasted_iota(jnp.int32, (extent, extent), 1)
            % extent
        )
        angle = grid.astype(jnp.float32) * (2.0 * math.pi / extent)
        tables_all.append((jnp.cos(angle), jnp.sin(angle)))
    grid = (
        lax.broadcasted_iota(jnp.int32, (outer_len, inner_len), 0)
        * lax.broadcasted_iota(jnp.int32, (outer_len, inner_len), 1)
        % padded_len
    )
    angle = grid.astype(jnp.float32) * (2.0 * math.pi / padded_len)
    tables_all.append((jnp.cos(angle)[:, :, None], jnp.sin(angle)[:, :, None]))
    return tables_all


def contract(form, left, right):
    return jnp.einsum(form, left, right, precision=lax.Precision.HIGHEST)


def forward_spectrum(signal, padded_len, tables_all):
    (cosine_outer, sine_outer), (cosine_inner, sine_inner), (twist_cos, twist_sin) = tables_all
    outer_len = cosine_outer.shape[0]
    used_outer = outer_len // 2
    length, chan_count = signal.shape
    cube = signal.reshape(used_outer, padded_len // outer_len, chan_count)
    real_first = contract("an,nmc->amc", cosine_outer[:, :used_outer], cube)
    imag_first = -contract("an,nmc->amc", sine_outer[:, :used_outer], cube)
    real_turn = real_first * twist_cos + imag_first * twist_sin
    imag_turn = imag_first * twist_cos - real_first * twist_sin
    real_spec = contract("amc,mb->abc", real_turn, cosine_inner) + contract(
        "amc,mb->abc", imag_turn, sine_inner
    )
    imag_spec = contract("amc,mb->abc", imag_turn, cosine_inner) - contract(
        "amc,mb->abc", real_turn, sine_inner
    )
    return (real_spec, imag_spec)


def inverse_spectrum(real_spec, imag_spec, padded_len, length, tables_all):
    (cosine_outer, sine_outer), (cosine_inner, sine_inner), (twist_cos, twist_sin) = tables_all
    used_outer = cosine_outer.shape[0] // 2
    real_mid = contract("abc,mb->amc", real_spec, cosine_inner) - contract(
        "abc,mb->amc", imag_spec, sine_inner
    )
    imag_mid = contract("abc,mb->amc", imag_spec, cosine_inner) + contract(
        "abc,mb->amc", real_spec, sine_inner
    )
    real_turn = real_mid * twist_cos - imag_mid * twist_sin
    imag_turn = imag_mid * twist_cos + real_mid * twist_sin
    signal = contract("na,amc->nmc", cosine_outer[:used_outer], real_turn) - contract(
        "na,amc->nmc", sine_outer[:used_outer], imag_turn
    )
    signal = signal / padded_len
    return signal.reshape(length, signal.shape[2])


def replicate_blocks(matrix, row_major, col_major, seq_devs):
    tok_rows = matrix.shape[0]
    block_width = matrix.shape[1] // (row_major if col_major == 1 else col_major)
    pieces = matrix.reshape(tok_rows, matrix.shape[1] // block_width, block_width).transpose(
        1, 0, 2
    )
    if col_major == 1:
        spread = jnp.broadcast_to(
            pieces[:, None], (row_major, seq_devs // row_major, tok_rows, block_width)
        )
    else:
        spread = jnp.broadcast_to(
            pieces[None], (seq_devs // col_major, col_major, tok_rows, block_width)
        )
    return spread.reshape(seq_devs, tok_rows, block_width)


def newton_step(current, gram):
    square = jnp.dot(gram, gram, precision=lax.Precision.HIGHEST)
    mixer = COEF_B * gram + COEF_C * square
    product = jnp.dot(mixer, current, precision=lax.Precision.HIGHEST)
    return COEF_A * current + product


def row_products(current):
    return lax.dot_general(
        current, current, (((1,), (1,)), ((), ())), precision=lax.Precision.HIGHEST
    )


def body(tokens, queries, keys, values, upstream, filters):
    seq_devs = lax.axis_size("seq")
    col_blocks = seq_devs // ROW_BLOCKS
    token_rep = replicate_blocks(tokens[0], ROW_BLOCKS, 1, seq_devs)
    key_wide = keys[0].astype(jnp.float32)
    value_wide = values[0].astype(jnp.float32)
    conv_grad = (upstream[0].astype(jnp.float32) * queries[0].astype(jnp.float32)).astype(
        jnp.bfloat16
    )
    gate_input = (key_wide * value_wide).astype(jnp.bfloat16)
    grad_chan, input_chan = (
        lax.all_to_all(conv_grad, "seq", split_axis=1, concat_axis=0, tiled=True),
        lax.all_to_all(gate_input, "seq", split_axis=1, concat_axis=0, tiled=True),
    )
    length = grad_chan.shape[0]
    padded_len = 2 * length
    outer_len = 2
    while padded_len % (outer_len * 2) == 0 and outer_len * 2 * (outer_len * 2) <= padded_len:
        outer_len = outer_len * 2
    tables_all = fourier_tables(padded_len, outer_len)
    filter_real, filter_imag = forward_spectrum(filters, padded_len, tables_all)
    grad_real, grad_imag = forward_spectrum(grad_chan.astype(jnp.float32), padded_len, tables_all)
    input_real, input_imag = forward_spectrum(
        input_chan.astype(jnp.float32), padded_len, tables_all
    )
    back_chan = inverse_spectrum(
        filter_real * grad_real + filter_imag * grad_imag,
        filter_real * grad_imag - filter_imag * grad_real,
        padded_len,
        length,
        tables_all,
    ).astype(jnp.bfloat16)
    filter_part = inverse_spectrum(
        grad_real * input_real + grad_imag * input_imag,
        grad_imag * input_real - grad_real * input_imag,
        padded_len,
        length,
        tables_all,
    )
    back_tok = lax.all_to_all(back_chan, "seq", split_axis=0, concat_axis=1, tiled=True)
    back_wide = back_tok.astype(jnp.float32)
    stacked = jnp.concatenate(
        [
            (back_wide * value_wide).astype(jnp.bfloat16),
            (back_wide * key_wide).astype(jnp.bfloat16),
        ],
        axis=1,
    )
    grad_rep = replicate_blocks(stacked, ROW_BLOCKS, col_blocks, seq_devs)
    token_blocks, grad_blocks = (
        lax.all_to_all(token_rep, "seq", split_axis=0, concat_axis=1, tiled=True),
        lax.all_to_all(grad_rep, "seq", split_axis=0, concat_axis=1, tiled=True),
    )
    partial_block = lax.dot_general(
        token_blocks[0],
        grad_blocks[0],
        (((0,), (0,)), ((), ())),
        preferred_element_type=jnp.float32,
    )
    filter_grad = lax.psum_scatter(filter_part, "dp", scatter_dimension=0, tiled=True)
    block_cols = partial_block.shape[1]
    half_block = lax.psum_scatter(partial_block, "dp", scatter_dimension=1, tiled=True)
    norm_sq = lax.psum(jnp.sum(half_block * half_block), "dp")
    current = half_block / (jnp.sqrt(norm_sq) + 1e-07)
    for iteration in range(NS_STEPS):
        gram = lax.psum(row_products(current), "dp")
        current = newton_step(current, gram)
    update = current * math.sqrt(block_cols)
    return (update[None], filter_grad)


def solution(mesh):
    return jax.shard_map(
        body,
        mesh=mesh,
        in_specs=(
            P("dp", "seq", None),
            P("dp", "seq", None),
            P("dp", "seq", None),
            P("dp", "seq", None),
            P("dp", "seq", None),
            P(None, "seq"),
        ),
        out_specs=(P("seq", None, "dp"), P("dp", "seq")),
        check_vma=False,
    )
```

profile of v0, /device:TPU:1, one launch (start us, length us, event | category | flops | bytes accessed | tf_op | source)
XLA Modules:
  0.0 925.2 jit_solution(11537930435930769156)
XLA Ops:
  11.7 10.3 %all-to-all-start.4 = ((bf16[128,64,64]{0,2,1:T(8,128)(2,1)}), bf16[128,64,64]{0,2,1:T(8,128)(2,1)S(1)}, u32[]{:S(2)}, u32[]{:S(2)}) async-start(bf16[128,64,64]{0,2,1:T(8,128)(2,1)} %bitcast.30), calls=%async_computation.5 | async-start | bytes 2097152 | tf_op jit(solution)/shard_map/all_to_all | solution.py:121
  42.3 6.1 convolution_add_fusion.2
  48.5 6.1 convolution_subtract_fusion.2
  60.9 9.2 all-to-all-start
  74.0 6.0 fusion.71
  80.0 6.2 fusion.72
  95.9 6.0 fusion.70
  102.0 6.6 convolution_add_fusion
  108.6 6.1 convolution_subtract_fusion
  114.7 6.2 convolution_add_fusion.1
  120.9 22.1 %multiply_add_fusion = (f32[128,128,64]{1,0,2:T(8,128)}, f32[128,128,64]{1,0,2:T(8,128)}, f32[128,128,64]{1,0,2:T(8,128)}, f32[128,128,64]{1,0,2:T(8,128)}) fusion(f32[128,128,64]{1,0,2:T(8,128)} %convolution_subtract_fusion, f32[128,128,64]{1,0,2:T(8,128)} %convolution_add_fusion.1, f32[128,128,64]{1,0,2:T(8,128)} %convolution_add_fusion, ...), kind=kOutput, calls=%fused_computation.33 | convolution fusion | flops 1628667904 | bytes 50462720 | tf_op jit(solution)/shard_map/amc,mb->abc/dot_general | solution.py:39
  143.0 9.4 %fusion.22 = f32[128,128,64]{0,1,2:T(8,128)S(1)} fusion(f32[128,128,64]{1,0,2:T(8,128)} %get-tuple-element.12), kind=kOutput, calls=%fused_computation.26 | convolution fusion | flops 1610842112 | bytes 8388608 | tf_op jit(solution)/shard_map/abc,mb->amc/dot_general | solution.py:39
  152.4 7.0 fusion.20
  159.5 7.1 fusion.28
  166.5 6.9 fusion.31
  181.4 7.8 all-to-all-start.1
  189.9 16.6 %all-to-all-done.1 = bf16[64,128,64]{1,2,0:T(8,128)(2,1)S(1)} async-done(((bf16[64,128,64]{1,2,0:T(8,128)(2,1)}), bf16[64,128,64]{1,2,0:T(8,128)(2,1)S(1)}, u32[]{:S(2)}, u32[]{:S(2)}) %all-to-all-start.1) | async-done | bytes 1048608 | tf_op jit(solution)/shard_map/all_to_all | solution.py:148
  217.5 106.0 %all-to-all-done.3 = bf16[64,128,512]{2,1,0:T(8,128)(2,1)} async-done(((bf16[64,128,512]{2,1,0:T(8,128)(2,1)}), bf16[64,128,512]{2,1,0:T(8,128)(2,1)}, u32[]{:S(2)}, u32[]{:S(2)}) %all-to-all-start.3) | async-done | bytes 8388640 | tf_op jit(solution)/shard_map/all_to_all | solution.py:159
  325.7 219.9 %all_to_all.54 = bf16[64,128,1024]{1,2,0:T(8,128)(2,1)S(1)} all-to-all(bf16[64,128,1024]{1,2,0:T(8,128)(2,1)S(1)} %bitcast.219), channel_id=1, replica_groups=mesh['seq'=64,'dp'=2] {'seq'}, dimensions={0} | all-to-all | bytes 33554432 | tf_op jit(solution)/shard_map/all_to_all | solution.py:160
  545.6 12.3 %convolution_bitcast_fusion = f32[512,1024]{0,1:T(8,128)} fusion(bf16[64,128,1024]{1,2,0:T(8,128)(2,1)S(1)} %all_to_all.54, bf16[64,128,512]{2,1,0:T(8,128)(2,1)} %all-to-all-done.3), kind=kOutput, calls=%fused_computation.68 | convolution fusion | flops 8589934592 | bytes 27262976 | tf_op jit(solution)/shard_map/dot_general | solution.py:162
  558.0 34.8 %reduce-scatter.3.cloned.1.call-done = f32[512,512]{0,1:T(8,128)} async-done(((f32[512,1024]{0,1:T(8,128)}), f32[512,512]{0,1:T(8,128)}) %reduce-scatter.3.cloned.1.call-update) | async-done | bytes 1048592 | tf_op jit(solution)/shard_map/reduce_scatter | solution.py:170
  594.9 6.1 psum.42
  606.3 48.7 %all-reduce.6.cloned.1.call-done = f32[512,512]{1,0:T(8,128)} async-done(((f32[512,512]{1,0:T(8,128)}), f32[512,512]{1,0:T(8,128)}) %all-reduce.6.cloned.1.call-update) | async-done | bytes 1048592 | tf_op jit(solution)/shard_map/psum | solution.py:174
  664.1 47.3 %all-reduce.8.cloned.1.call-done = f32[512,512]{1,0:T(8,128)} async-done(((f32[512,512]{1,0:T(8,128)}), f32[512,512]{1,0:T(8,128)}) %all-reduce.8.cloned.1.call-update) | async-done | bytes 1048592 | tf_op jit(solution)/shard_map/psum | solution.py:174
  720.1 47.5 %all-reduce.10.cloned.1.call-done = f32[512,512]{1,0:T(8,128)} async-done(((f32[512,512]{1,0:T(8,128)}), f32[512,512]{1,0:T(8,128)}) %all-reduce.10.cloned.1.call-update) | async-done | bytes 1048592 | tf_op jit(solution)/shard_map/psum | solution.py:174
  776.7 9.3 %fusion.8 = f32[128,128,64]{0,1,2:T(8,128)S(1)} fusion(f32[128,128,64]{1,0,2:T(8,128)} %get-tuple-element.9), kind=kOutput, calls=%fused_computation.10 | convolution fusion | flops 1610842112 | bytes 8388608 | tf_op jit(solution)/shard_map/abc,mb->amc/dot_general | solution.py:39
  786.1 8.7 fusion.6
  794.7 8.9 fusion.34
  803.6 20.2 %all-reduce.12.cloned.1.call-done = f32[512,512]{1,0:T(8,128)} async-done(((f32[512,512]{1,0:T(8,128)}), f32[512,512]{1,0:T(8,128)}) %all-reduce.12.cloned.1.call-update) | async-done | bytes 1048592 | tf_op jit(solution)/shard_map/psum | solution.py:174
  832.5 9.8 %fusion.37 = f32[128,128,64]{0,1,2:T(8,128)S(1)} fusion(f32[128,128,64]{0,1,2:T(8,128)} %fusion.6, f32[128,128,64]{1,0,2:T(8,128)} %get-tuple-element.8), kind=kOutput, calls=%fused_computation.45 | convolution fusion | flops 1611890688 | bytes 12582912 | tf_op jit(solution)/shard_map/abc,mb->amc/dot_general | solution.py:39
  850.6 29.4 %all-reduce.14.cloned.1.call-done = f32[512,512]{1,0:T(8,128)} async-done(((f32[512,512]{1,0:T(8,128)}), f32[512,512]{1,0:T(8,128)}) %all-reduce.14.cloned.1.call-update) | async-done | bytes 1048592 | tf_op jit(solution)/shard_map/psum | solution.py:174
  887.4 30.8 %reduce-scatter.5.cloned.1.call-done = f32[4096,64]{0,1:T(8,128)} async-done(((f32[8192,64]{0,1:T(8,128)}), f32[4096,64]{0,1:T(8,128)}) %reduce-scatter.5.cloned.1.call-update) | async-done | bytes 1048592 | tf_op jit(solution)/shard_map/reduce_scatter | solution.py:168
  (103 shorter events, 124.3 us)
Async XLA Ops:
  10.4 1.3 copy-start.13
  11.7 49.2 %all-to-all-start.4 = ((bf16[128,64,64]{0,2,1:T(8,128)(2,1)}), bf16[128,64,64]{0,2,1:T(8,128)(2,1)S(1)}, u32[]{:S(2)}, u32[]{:S(2)}) async-start(bf16[128,64,64]{0,2,1:T(8,128)(2,1)} %bitcast.30), calls=%async_computation.5 | async-start | bytes 2097152 | tf_op jit(solution)/shard_map/all_to_all | solution.py:121
  60.9 26.4 %all-to-all-start = ((bf16[128,64,64]{0,2,1:T(8,128)(2,1)}), bf16[128,64,64]{0,2,1:T(8,128)(2,1)S(1)}, u32[]{:S(2)}, u32[]{:S(2)}) async-start(bf16[128,64,64]{0,2,1:T(8,128)(2,1)} %bitcast.228), calls=%async_computation | async-start | bytes 2097152 | tf_op jit(solution)/shard_map/all_to_all | solution.py:120
  72.0 8.0 copy-start.2
  74.0 6.1 copy-start.4
  89.3 25.4 %copy-start = (f32[128,128,64]{1,0,2:T(8,128)}, f32[128,128,64]{1,0,2:T(8,128)S(1)}, u32[]{:S(2)}) copy-start(f32[128,128,64]{1,0,2:T(8,128)S(1)} %fusion.63) | copy-start | bytes 12582916
  91.2 23.5 %copy-start.1 = (f32[128,128,64]{1,0,2:T(8,128)}, f32[128,128,64]{1,0,2:T(8,128)S(1)}, u32[]{:S(2)}) copy-start(f32[128,128,64]{1,0,2:T(8,128)S(1)} %fusion.65) | copy-start | bytes 12582916
  95.9 6.1 copy-start.3
  95.9 6.1 copy-start.5
  95.9 6.1 copy-start.12
  102.0 6.6 copy-start.11
  143.0 9.4 %copy-start.10 = (f32[128,128,64]{1,0,2:T(8,128)S(1)}, f32[128,128,64]{1,0,2:T(8,128)}, u32[]{:S(2)}) copy-start(f32[128,128,64]{1,0,2:T(8,128)} %get-tuple-element.12) | copy-start | bytes 12582916
  152.4 7.1 copy-start.7
  179.7 9.5 %copy-start.15 = (bf16[1,128,4096]{2,1,0:T(8,128)(2,1)S(1)}, bf16[1,128,4096]{2,1,0:T(8,128)(2,1)}, u32[]{:S(2)}) copy-start(bf16[1,128,4096]{2,1,0:T(8,128)(2,1)} %param.6) | copy-start | bytes 3145732
  181.4 25.2 %all-to-all-start.1 = ((bf16[64,128,64]{1,2,0:T(8,128)(2,1)}), bf16[64,128,64]{1,2,0:T(8,128)(2,1)S(1)}, u32[]{:S(2)}, u32[]{:S(2)}) async-start(bf16[64,128,64]{1,2,0:T(8,128)(2,1)} %copy.109), calls=%async_computation.1 | async-start | bytes 2097152 | tf_op jit(solution)/shard_map/all_to_all | solution.py:148
  210.8 6.1 copy-start.14
  210.8 112.7 %all-to-all-start.3 = ((bf16[64,128,512]{2,1,0:T(8,128)(2,1)}), bf16[64,128,512]{2,1,0:T(8,128)(2,1)}, u32[]{:S(2)}, u32[]{:S(2)}) async-start(bf16[64,128,512]{2,1,0:T(8,128)(2,1)} %bitcast.220), calls=%async_computation.3 | async-start | bytes 16777216 | tf_op jit(solution)/shard_map/all_to_all | solution.py:159
  216.5 376.3 %reduce-scatter.3.cloned.1.call-start = ((), (), s32[]{:S(2)}) async-start(), calls=%async_computation.7 | async-start | bytes 3145728 | tf_op jit(solution)/shard_map/reduce_scatter | solution.py:170
  557.9 97.1 %all-reduce.6.cloned.1.call-start = ((), (), s32[]{:S(2)}) async-start(), calls=%async_computation.8 | async-start | bytes 2097152 | tf_op jit(solution)/shard_map/psum | solution.py:174
  601.7 57.4 %copy-start.16 = (f32[512,512]{0,1:T(8,128)S(1)}, f32[512,512]{0,1:T(8,128)}, u32[]{:S(2)}) copy-start(f32[512,512]{0,1:T(8,128)} %reduce-scatter.3.cloned.1.call-done) | copy-start | bytes 3145732
  606.2 105.2 %all-reduce.8.cloned.1.call-start = ((), (), s32[]{:S(2)}) async-start(), calls=%async_computation.9 | async-start | bytes 2097152 | tf_op jit(solution)/shard_map/psum | solution.py:174
  663.8 103.8 %all-reduce.10.cloned.1.call-start = ((), (), s32[]{:S(2)}) async-start(), calls=%async_computation.10 | async-start | bytes 2097152 | tf_op jit(solution)/shard_map/psum | solution.py:174
  720.1 103.8 %all-reduce.12.cloned.1.call-start = ((), (), s32[]{:S(2)}) async-start(), calls=%async_computation.11 | async-start | bytes 2097152 | tf_op jit(solution)/shard_map/psum | solution.py:174
  776.2 103.8 %all-reduce.14.cloned.1.call-start = ((), (), s32[]{:S(2)}) async-start(), calls=%async_computation.12 | async-start | bytes 2097152 | tf_op jit(solution)/shard_map/psum | solution.py:174
  776.7 9.4 %copy-start.8 = (f32[128,128,64]{1,0,2:T(8,128)S(1)}, f32[128,128,64]{1,0,2:T(8,128)}, u32[]{:S(2)}) copy-start(f32[128,128,64]{1,0,2:T(8,128)} %get-tuple-element.9) | copy-start | bytes 12582916
  786.1 8.7 copy-start.6
  832.5 85.7 %reduce-scatter.5.cloned.1.call-start = ((), (), s32[]{:S(2)}) async-start(), calls=%async_computation.13 | async-start | bytes 3145728 | tf_op jit(solution)/shard_map/reduce_scatter | solution.py:168
  832.5 9.8 %copy-start.9 = (f32[128,128,64]{0,1,2:T(8,128)S(1)}, f32[128,128,64]{0,1,2:T(8,128)}, u32[]{:S(2)}) copy-start(f32[128,128,64]{0,1,2:T(8,128)} %fusion.34) | copy-start | bytes 12582916
Sparse Core Ops, SparseCore 0:
  558.0 34.7 reduce-scatter.2
  606.4 48.5 all-reduce.5
  664.0 47.3 all-reduce.7
  720.2 47.3 all-reduce.9
  776.4 47.3 all-reduce.11
  832.6 47.3 all-reduce.13
  882.9 35.1 reduce-scatter.4
where the time goes:
time: 936 us; the launch traced here: 925 us
  waiting for transfers between devices  382 us (41%)
  matrix products  237 us (25%)
  blocking collectives  226 us (24%)
  starting transfers between devices  34 us (4%)
  local copies, waits for them, and re-layouts  22.1 us (2%)
  between operations  15.6 us (2%)
    all_to_all x1, blocking collectives, body(): lax.all_to_all(grad_rep, 'seq', split_axis=0, concat_axis=1, tiled=True)  220 us
    psum x5, waiting for transfers between devices, body(): gram = lax.psum(row_products(current), 'dp')  193 us
    dot_general x30, matrix products, contract(): return jnp.einsum(form, left, right, precision=lax.Precision.HIGHEST)  180 us
    all_to_all x1, waiting for transfers between devices, body(): lax.all_to_all(token_rep, 'seq', split_axis=0, concat_axis=1, tiled=True)  106 us
    reduce_scatter x1, waiting for transfers between devices, body(): lax.psum_scatter(partial_block, 'dp', scatter_dimension=1, tiled=True)  34.8 us
    reduce_scatter x1, waiting for transfers between devices, body(): lax.psum_scatter(filter_part, 'dp', scatter_dimension=0, tiled=True)  30.8 us
    dot_general x5, matrix products, newton_step(): square = jnp.dot(gram, gram, precision=lax.Precision.HIGHEST)  20 us
  transfers between devices with their start and end apart: 11, of which 10 were waited for; matrix products, arithmetic and copies ran while one was open for 12% of the time, Pallas kernels for 0%

commit v1 on v0

--- a/solution.py
+++ b/solution.py
@@ -36,7 +36,7 @@
 
 
 def contract(form, left, right):
-    return jnp.einsum(form, left, right, precision=lax.Precision.HIGHEST)
+    return jnp.einsum(form, left, right, precision=lax.Precision.HIGH)
 
 
 def forward_spectrum(signal, padded_len, tables_all):
@@ -93,11 +93,15 @@
     return spread.reshape(seq_devs, tok_rows, block_width)
 
 
-def newton_step(current, gram):
-    square = jnp.dot(gram, gram, precision=lax.Precision.HIGHEST)
+def newton_step(current, gram, last):
+    square = jnp.dot(gram, gram, precision=lax.Precision.HIGH)
     mixer = COEF_B * gram + COEF_C * square
-    product = jnp.dot(mixer, current, precision=lax.Precision.HIGHEST)
-    return COEF_A * current + product
+    moved = COEF_A * current + jnp.dot(mixer, current, precision=lax.Precision.HIGH)
+    if last:
+        return moved, None
+    half = COEF_A * gram + jnp.dot(mixer, gram, precision=lax.Precision.HIGH)
+    following = COEF_A * half + jnp.dot(half, mixer, precision=lax.Precision.HIGH)
+    return moved, following
 
 
 def row_products(current):
@@ -168,11 +172,12 @@
     filter_grad = lax.psum_scatter(filter_part, "dp", scatter_dimension=0, tiled=True)
     block_cols = partial_block.shape[1]
     half_block = lax.psum_scatter(partial_block, "dp", scatter_dimension=1, tiled=True)
-    norm_sq = lax.psum(jnp.sum(half_block * half_block), "dp")
-    current = half_block / (jnp.sqrt(norm_sq) + 1e-07)
+    raw_gram = lax.psum(row_products(half_block), "dp")
+    norm = jnp.sqrt(jnp.trace(raw_gram)) + 1e-07
+    current = half_block / norm
+    gram = raw_gram / (norm * norm)
     for iteration in range(NS_STEPS):
-        gram = lax.psum(row_products(current), "dp")
-        current = newton_step(current, gram)
+        current, gram = newton_step(current, gram, iteration == NS_STEPS - 1)
     update = current * math.sqrt(block_cols)
     return (update[None], filter_grad)
 

time: 936 us -> 669 us (0.71)
  waiting for transfers between devices: 382 us -> 193 us
  matrix products: 237 us -> 168 us
    psum x5 -> x1, waiting for transfers between devices: 193 us -> 34.3 us  [body(): raw_gram = lax.psum(row_products(half_block), 'dp')]
    dot_general x40 -> x48, matrix products: 209 us -> 152 us  [the longest x30 131 us: contract(): return jnp.einsum(form, left, right, precision=lax.Precision.HIGH)]
    reduce_scatter x1, waiting for transfers between devices: 30.8 us -> 13 us  [body(): lax.psum_scatter(filter_part, 'dp', scatter_dimension=0, tiled=True)]
    reduce_scatter x1, waiting for transfers between devices: 34.8 us -> 18 us  [body(): lax.psum_scatter(partial_block, 'dp', scatter_dimension=1, tiled=True)]
    dot_general x5 -> x1, matrix products: 15.9 us -> 4.41 us  [row_products(): lax.dot_general(current, current, (((1,), (1,)), ((), ())), precision=lax...]
  transfers between devices with their start and end apart: 11 -> 7, of which waited for: 10 -> 6; matrix products, arithmetic and copies ran while one was open for 12% -> 16% of each run, Pallas kernels for 0% -> 0%
where the time goes in v1:
time: 669 us; the launch traced here: 658 us
  blocking collectives  220 us (33%)
  waiting for transfers between devices  193 us (29%)
  matrix products  168 us (25%)
  starting transfers between devices  30.1 us (4%)
  local copies, waits for them, and re-layouts  23.6 us (4%)
  between operations  15.5 us (2%)
  other arithmetic  7.56 us (1%)
    all_to_all x1, blocking collectives, body(): lax.all_to_all(grad_rep, 'seq', split_axis=0, concat_axis=1, tiled=True)  220 us
    dot_general x30, matrix products, contract(): return jnp.einsum(form, left, right, precision=lax.Precision.HIGH)  131 us
    all_to_all x1, waiting for transfers between devices, body(): lax.all_to_all(token_rep, 'seq', split_axis=0, concat_axis=1, tiled=True)  106 us
    psum x1, waiting for transfers between devices, body(): raw_gram = lax.psum(row_products(half_block), 'dp')  34.3 us
    reduce_scatter x1, waiting for transfers between devices, body(): lax.psum_scatter(partial_block, 'dp', scatter_dimension=1, tiled=True)  18 us
    all_to_all x1, waiting for transfers between devices, body(): lax.all_to_all(back_chan, 'seq', split_axis=0, concat_axis=1, tiled=True)  16.6 us
    unnamed x44, local copies, waits for them, and re-layouts  14.9 us
  transfers between devices with their start and end apart: 7, of which 6 were waited for; matrix products, arithmetic and copies ran while one was open for 16% of the time, Pallas kernels for 0%

profile of v1, /device:TPU:1, one launch (start us, length us, event | category | flops | bytes accessed | tf_op | source)
XLA Modules:
  0.0 658.3 jit_solution(11263309453823892289)
XLA Ops:
  11.7 10.3 %all-to-all-start.4 = ((bf16[128,64,64]{0,2,1:T(8,128)(2,1)}), bf16[128,64,64]{0,2,1:T(8,128)(2,1)S(1)}, u32[]{:S(2)}, u32[]{:S(2)}) async-start(bf16[128,64,64]{0,2,1:T(8,128)(2,1)} %bitcast.30), calls=%async_computation.5 | async-start | bytes 2097152 | tf_op jit(solution)/shard_map/all_to_all | solution.py:125
  34.5 16.0 %convolution_add_fusion.2 = f32[128,128,64]{1,0,2:T(8,128)} fusion(f32[128,128,64]{1,0,2:T(8,128)S(1)} %fusion.68, f32[128,128,64]{1,0,2:T(8,128)S(1)} %fusion.134, f32[128,128,64]{1,0,2:T(8,128)S(1)} %fusion.135, f32[128,128]{1,0:T(8,128)S(1)} %copy.117, f32[128,128]{1,0:T(8,128)S(1)} %copy.116), kind=kOutput, calls=%fused_computation.51 | convolution fusion | flops 810778624 | bytes 16908288 | tf_op jit(solution)/shard_map/amc,mb->abc/dot_general | solution.py:39
  50.5 4.4 convolution_subtract_fusion.2
  61.3 8.9 %all-to-all-start = ((bf16[128,64,64]{0,2,1:T(8,128)(2,1)}), bf16[128,64,64]{0,2,1:T(8,128)(2,1)S(1)}, u32[]{:S(2)}, u32[]{:S(2)}) async-start(bf16[128,64,64]{0,2,1:T(8,128)(2,1)} %bitcast.235), calls=%async_computation | async-start | bytes 2097152 | tf_op jit(solution)/shard_map/all_to_all | solution.py:124
  73.2 4.5 fusion.72
  77.7 4.4 fusion.73
  82.1 5.4 all-to-all-done
  93.8 4.6 fusion.71
  99.9 4.5 convolution_add_fusion
  104.4 4.4 convolution_subtract_fusion
  108.8 4.5 convolution_add_fusion.1
  113.3 17.5 %multiply_add_fusion = (f32[128,128,64]{1,0,2:T(8,128)}, f32[128,128,64]{1,0,2:T(8,128)}, f32[128,128,64]{1,0,2:T(8,128)}, f32[128,128,64]{1,0,2:T(8,128)}) fusion(f32[128,128,64]{1,0,2:T(8,128)} %convolution_subtract_fusion, f32[128,128,64]{1,0,2:T(8,128)} %convolution_add_fusion.1, f32[128,128,64]{1,0,2:T(8,128)} %convolution_add_fusion, ...), kind=kOutput, calls=%fused_computation.33 | convolution fusion | flops 823361536 | bytes 50462720 | tf_op jit(solution)/shard_map/amc,mb->abc/dot_general | solution.py:39
  130.8 5.9 fusion.22
  136.7 3.7 fusion.20
  140.4 3.6 fusion.28
  144.0 3.6 fusion.31
  152.7 4.8 all-to-all-start.1
  158.3 16.6 %all-to-all-done.1 = bf16[64,128,64]{1,2,0:T(8,128)(2,1)S(1)} async-done(((bf16[64,128,64]{1,2,0:T(8,128)(2,1)}), bf16[64,128,64]{1,2,0:T(8,128)(2,1)S(1)}, u32[]{:S(2)}, u32[]{:S(2)}) %all-to-all-start.1) | async-done | bytes 1048608 | tf_op jit(solution)/shard_map/all_to_all | solution.py:152
  174.9 4.2 broadcast_in_dim.10
  179.1 5.8 all-to-all-start.3
  185.8 106.0 %all-to-all-done.3 = bf16[64,128,512]{2,1,0:T(8,128)(2,1)} async-done(((bf16[64,128,512]{2,1,0:T(8,128)(2,1)}), bf16[64,128,512]{2,1,0:T(8,128)(2,1)}, u32[]{:S(2)}, u32[]{:S(2)}) %all-to-all-start.3) | async-done | bytes 8388640 | tf_op jit(solution)/shard_map/all_to_all | solution.py:163
  294.1 219.9 %all_to_all.54 = bf16[64,128,1024]{1,2,0:T(8,128)(2,1)S(1)} all-to-all(bf16[64,128,1024]{1,2,0:T(8,128)(2,1)S(1)} %bitcast.226), channel_id=1, replica_groups=mesh['seq'=64,'dp'=2] {'seq'}, dimensions={0} | all-to-all | bytes 33554432 | tf_op jit(solution)/shard_map/all_to_all | solution.py:164
  514.0 12.2 %convolution_bitcast_fusion = f32[512,1024]{0,1:T(8,128)} fusion(bf16[64,128,1024]{1,2,0:T(8,128)(2,1)S(1)} %all_to_all.54, bf16[64,128,512]{2,1,0:T(8,128)(2,1)} %all-to-all-done.3), kind=kOutput, calls=%fused_computation.68 | convolution fusion | flops 8589934592 | bytes 27262976 | tf_op jit(solution)/shard_map/dot_general | solution.py:166
  526.3 6.3 fusion.8
  532.6 5.3 fusion.6
  537.9 5.3 fusion.34
  543.2 18.0 %reduce-scatter.3.cloned.1.call-done = f32[512,512]{0,1:T(8,128)} async-done(((f32[512,1024]{0,1:T(8,128)}), f32[512,512]{0,1:T(8,128)}) %reduce-scatter.3.cloned.1.call-update) | async-done | bytes 1048592 | tf_op jit(solution)/shard_map/reduce_scatter | solution.py:174
  561.1 4.4 fusion.216
  565.8 7.2 %fusion.37 = f32[128,128,64]{0,1,2:T(8,128)S(1)} fusion(f32[128,128,64]{0,1,2:T(8,128)} %fusion.6, f32[128,128,64]{1,0,2:T(8,128)} %get-tuple-element.8), kind=kOutput, calls=%fused_computation.45 | convolution fusion | flops 806584320 | bytes 12582912 | tf_op jit(solution)/shard_map/abc,mb->amc/dot_general | solution.py:39
  578.8 34.3 %all-reduce.2.cloned.1.call-done = f32[512,512]{0,1:T(8,128)} async-done(((f32[512,512]{0,1:T(8,128)}), f32[512,512]{0,1:T(8,128)}) %all-reduce.2.cloned.1.call-update) | async-done | bytes 1048592 | tf_op jit(solution)/shard_map/psum | solution.py:175
  615.7 3.3 fusion.58
  638.3 13.0 %reduce-scatter.5.cloned.1.call-done = f32[4096,64]{0,1:T(8,128)} async-done(((f32[8192,64]{0,1:T(8,128)}), f32[4096,64]{0,1:T(8,128)}) %reduce-scatter.5.cloned.1.call-update) | async-done | bytes 1048592 | tf_op jit(solution)/shard_map/reduce_scatter | solution.py:172
  (96 shorter events, 70.1 us)
Async XLA Ops:
  10.4 1.3 copy-start.13
  11.7 49.6 %all-to-all-start.4 = ((bf16[128,64,64]{0,2,1:T(8,128)(2,1)}), bf16[128,64,64]{0,2,1:T(8,128)(2,1)S(1)}, u32[]{:S(2)}, u32[]{:S(2)}) async-start(bf16[128,64,64]{0,2,1:T(8,128)(2,1)} %bitcast.30), calls=%async_computation.5 | async-start | bytes 2097152 | tf_op jit(solution)/shard_map/all_to_all | solution.py:125
  61.3 26.2 %all-to-all-start = ((bf16[128,64,64]{0,2,1:T(8,128)(2,1)}), bf16[128,64,64]{0,2,1:T(8,128)(2,1)S(1)}, u32[]{:S(2)}, u32[]{:S(2)}) async-start(bf16[128,64,64]{0,2,1:T(8,128)(2,1)} %bitcast.235), calls=%async_computation | async-start | bytes 2097152 | tf_op jit(solution)/shard_map/all_to_all | solution.py:124
  71.7 6.0 copy-start.2
  73.2 4.5 copy-start.4
  89.1 19.7 %copy-start = (f32[128,128,64]{1,0,2:T(8,128)}, f32[128,128,64]{1,0,2:T(8,128)S(1)}, u32[]{:S(2)}) copy-start(f32[128,128,64]{1,0,2:T(8,128)S(1)} %fusion.63) | copy-start | bytes 12582916
  90.7 18.2 %copy-start.1 = (f32[128,128,64]{1,0,2:T(8,128)}, f32[128,128,64]{1,0,2:T(8,128)S(1)}, u32[]{:S(2)}) copy-start(f32[128,128,64]{1,0,2:T(8,128)S(1)} %fusion.65) | copy-start | bytes 12582916
  93.7 4.6 copy-start.3
  93.7 4.6 copy-start.5
  93.7 6.2 copy-start.12
  99.9 4.5 copy-start.11
  130.8 5.9 copy-start.10
  136.7 3.7 copy-start.7
  151.1 6.5 copy-start.16
  152.7 22.2 %all-to-all-start.1 = ((bf16[64,128,64]{1,2,0:T(8,128)(2,1)}), bf16[64,128,64]{1,2,0:T(8,128)(2,1)S(1)}, u32[]{:S(2)}, u32[]{:S(2)}) async-start(bf16[64,128,64]{1,2,0:T(8,128)(2,1)} %copy.135), calls=%async_computation.1 | async-start | bytes 2097152 | tf_op jit(solution)/shard_map/all_to_all | solution.py:152
  179.1 6.1 copy-start.14
  179.1 112.7 %all-to-all-start.3 = ((bf16[64,128,512]{2,1,0:T(8,128)(2,1)}), bf16[64,128,512]{2,1,0:T(8,128)(2,1)}, u32[]{:S(2)}, u32[]{:S(2)}) async-start(bf16[64,128,512]{2,1,0:T(8,128)(2,1)} %bitcast.227), calls=%async_computation.3 | async-start | bytes 16777216 | tf_op jit(solution)/shard_map/all_to_all | solution.py:163
  184.9 376.2 %reduce-scatter.3.cloned.1.call-start = ((), (), s32[]{:S(2)}) async-start(), calls=%async_computation.7 | async-start | bytes 3145728 | tf_op jit(solution)/shard_map/reduce_scatter | solution.py:174
  526.3 86.9 %all-reduce.2.cloned.1.call-start = ((), (), s32[]{:S(2)}) async-start(), calls=%async_computation.8 | async-start | bytes 2097152 | tf_op jit(solution)/shard_map/psum | solution.py:175
  526.3 6.3 copy-start.8
  532.6 5.3 copy-start.6
  565.6 85.7 %reduce-scatter.5.cloned.1.call-start = ((), (), s32[]{:S(2)}) async-start(), calls=%async_computation.9 | async-start | bytes 3145728 | tf_op jit(solution)/shard_map/reduce_scatter | solution.py:172
  565.8 7.2 %copy-start.9 = (f32[128,128,64]{0,1,2:T(8,128)S(1)}, f32[128,128,64]{0,1,2:T(8,128)}, u32[]{:S(2)}) copy-start(f32[128,128,64]{0,1,2:T(8,128)} %fusion.34) | copy-start | bytes 12582916
  615.7 3.3 copy-start.17
  620.1 3.3 copy-start.15
Sparse Core Ops, SparseCore 0:
  526.4 34.7 reduce-scatter.2
  565.7 47.3 all-reduce.1
  616.1 35.1 reduce-scatter.4

commit v2 on v0

v2 whole, which is shorter than its diff:
```python
import math

import jax
import jax.numpy as jnp
import numpy as np
from jax import lax
from jax.experimental import pallas as pl
from jax.experimental.pallas import tpu as pltpu
from jax.sharding import PartitionSpec as P

F32, BF16 = jnp.float32, jnp.bfloat16
RADIX = 128
HALF = 64
NS_STEPS = 5
COEF_A = 3.4445
COEF_B = -4.775
COEF_C = 2.0315
ROWS = 72


def split_table(table):
    high = np.asarray(table, np.float32).astype(jnp.bfloat16)
    low = (np.asarray(table, np.float64) - high.astype(np.float64)).astype(jnp.bfloat16)
    return high, low


def fourier_tables():
    total = RADIX * RADIX
    spot = np.arange(RADIX)
    used = np.arange(HALF + 1)
    outer = 2.0 * math.pi * (np.outer(used, np.arange(HALF)) % RADIX) / RADIX
    first = np.zeros((2 * ROWS, HALF))
    first[: HALF + 1] = np.cos(outer)
    first[ROWS : ROWS + HALF + 1] = -np.sin(outer)
    weight = np.where((used == 0) | (used == HALF), 1.0, 2.0)[:, None] / total
    last = np.zeros((2 * ROWS, HALF))
    last[: HALF + 1] = np.cos(outer) * weight
    last[ROWS : ROWS + HALF + 1] = -np.sin(outer) * weight
    last = last.T
    inner = 2.0 * math.pi * (np.outer(spot, spot) % RADIX) / RADIX
    real, imag = np.cos(inner), -np.sin(inner)
    forward = np.block([[real, imag], [-imag, real]])
    turn = 2.0 * math.pi * np.outer(used, spot) / total
    twist = np.zeros((2, ROWS, RADIX), np.float32)
    twist[0, : HALF + 1] = np.cos(turn)
    twist[1, : HALF + 1] = -np.sin(turn)
    first_high, first_low = split_table(first)
    last_high, last_low = split_table(last)
    ahead_high, ahead_low = split_table(forward)
    back_high, back_low = split_table(forward.T)
    return (
        np.concatenate([first_high, first_low, first_high], 1),
        np.concatenate([ahead_high, ahead_high, ahead_low], 0),
        np.concatenate([back_high, back_high, back_low], 0),
        np.concatenate([last_high, last_low, last_high], 1),
        twist,
    )


def dot(left, right):
    return jnp.dot(left, right, preferred_element_type=F32)


def parts(value):
    high = value.astype(BF16)
    return high, (value - high.astype(F32)).astype(BF16)


def convolve_pair(grads, inputs, filters, tables):
    first_ref, ahead_ref, back_ref, last_ref, twist_ref = tables
    turn_real, turn_imag = twist_ref[0], twist_ref[1]
    signals = jnp.concatenate([grads[0], inputs[0], grads[1], inputs[1]], axis=1)
    signals = jnp.concatenate([signals, signals], axis=0)
    spread = dot(first_ref[:, : 2 * HALF], signals)
    high, low = parts(jnp.concatenate(filters, axis=1))
    spread_filter = dot(first_ref[...], jnp.concatenate([high, high, low], axis=0))
    turned = []
    for block in (spread, spread_filter):
        for at in range(0, block.shape[1], RADIX):
            real, imag = block[:ROWS, at : at + RADIX], block[ROWS:, at : at + RADIX]
            turned.append(
                jnp.concatenate(
                    [real * turn_real - imag * turn_imag, real * turn_imag + imag * turn_real], axis=1
                )
            )
    high, low = parts(jnp.concatenate(turned, axis=0))
    spectra = dot(jnp.concatenate([high, low, high], axis=1), ahead_ref[...])
    spec = [
        (spectra[i * ROWS : (i + 1) * ROWS, :RADIX], spectra[i * ROWS : (i + 1) * ROWS, RADIX:])
        for i in range(6)
    ]
    products = []
    for which in range(2):
        grad_real, grad_imag = spec[2 * which]
        input_real, input_imag = spec[2 * which + 1]
        filter_real, filter_imag = spec[4 + which]
        for other_real, other_imag, flip in (
            (filter_real, filter_imag, 0),
            (input_real, input_imag, 0),
        ):
            products.append(
                jnp.concatenate(
                    [
                        grad_real * other_real + grad_imag * other_imag,
                        grad_imag * other_real - grad_real * other_imag,
                    ],
                    axis=1,
                )
            )
    high, low = parts(jnp.concatenate(products, axis=0))
    mixed = dot(jnp.concatenate([high, low, high], axis=1), back_ref[...])
    columns = []
    for i in range(4):
        real, imag = mixed[i * ROWS : (i + 1) * ROWS, :RADIX], mixed[i * ROWS : (i + 1) * ROWS, RADIX:]
        columns.append(
            jnp.concatenate(
                [real * turn_real + imag * turn_imag, imag * turn_real - real * turn_imag], axis=0
            )
        )
    high, low = parts(jnp.concatenate(columns, axis=1))
    result = dot(last_ref[...], jnp.concatenate([high, high, low], axis=0))
    return [result[:, i * RADIX : (i + 1) * RADIX] for i in range(4)]


GROUP = 16


def conv_group(at, g_ref, k_ref, v_ref, f_ref, fg_ref, key_rows, value_rows, tables):
    def pair(j, carry):
        chans = [at + 2 * j, at + 2 * j + 1]
        keys = [k_ref[c].astype(F32) for c in chans]
        values = [v_ref[c].astype(F32) for c in chans]
        inputs = [(a * b).astype(BF16) for a, b in zip(keys, values)]
        out = convolve_pair([g_ref[c] for c in chans], inputs, [f_ref[c] for c in chans], tables)
        for i in range(2):
            back = out[2 * i].astype(BF16).astype(F32)
            fg_ref[chans[i]] = out[2 * i + 1]
            key_rows[pl.ds(2 * j + i, HALF, stride=GROUP), :] = back * values[i]
            value_rows[pl.ds(2 * j + i, HALF, stride=GROUP), :] = back * keys[i]
        return carry

    lax.fori_loop(0, GROUP // 2, pair, 0)


def place():
    me = lax.axis_index("seq")
    return me // 32, me // 8 % 4, me // 2 % 4, me % 2


def seq_of(z, x, y, c):
    return ((z * 4 + x) * 4 + y) * 2 + c


def remote(src, dst, send, recv, **device):
    return pltpu.make_async_remote_copy(
        src_ref=src,
        dst_ref=dst,
        send_sem=send,
        recv_sem=recv,
        device_id=device,
        device_id_type=pl.DeviceIdType.MESH,
    )


GROUPS = 4
PIECES = 32


def gradient_kernel(
    g_ref, k_ref, v_ref, f_ref, tok_ref, t0, t1, t2, t3, t4,
    part_ref, fg_ref,
    tok, cols, own, fg_all, fg_in, key_rows, value_rows,
    tok_first, tok_first_send, tok_recv, tok_send, col_recv, col_send, fg_sem,
):
    tables = (t0, t1, t2, t3, t4)
    z, x, y, c = place()
    dp = lax.axis_index("dp")
    up, down, across = (y + 1) % 4, (y + 3) % 4, (y + 2) % 4
    right, left, far = (x + 1) % 4, (x + 3) % 4, (x + 2) % 4
    sibling = seq_of(z, x, y, 1 - c)
    x_right, x_left = seq_of(z, right, y, c), seq_of(z, left, y, c)
    z_other = seq_of(1 - z, x, y, c)

    barrier = pltpu.get_barrier_semaphore()
    friends = [
        seq_of(z, x, up, 0), seq_of(z, x, up, 1), seq_of(z, x, down, 0), seq_of(z, x, down, 1),
        seq_of(z, x, across, c), x_right, x_left, z_other, sibling,
    ]
    for friend in friends:
        pl.semaphore_signal(
            barrier, inc=1, device_id={"seq": friend}, device_id_type=pl.DeviceIdType.MESH
        )
    pl.semaphore_signal(barrier, inc=1, device_id={"dp": 1 - dp}, device_id_type=pl.DeviceIdType.MESH)
    pl.semaphore_wait(barrier, len(friends) + 1)

    pending = []

    def launch(copy):
        copy.start()
        pending.append(copy)

    here = z * 4 + x
    first = []
    for i, target in enumerate((up, down, across)):
        copy = remote(
            tok_ref.at[target], tok.at[here, c, y], tok_first_send.at[i], tok_first.at[i],
            seq=seq_of(z, x, target, c),
        )
        launch(copy)
        first.append(copy)
    local_first = pltpu.make_async_copy(tok_ref.at[y], tok.at[here, c, y], tok_first.at[3])
    local_first.start()

    count = [0]

    def half(zz, xx, cc, h):
        return tok.at[zz * 4 + xx, cc, pl.ds(2 * h, 2)]

    def send_half(zz, xx, h, target):
        launch(
            remote(
                half(zz, xx, c, h), half(zz, xx, c, h), tok_send.at[count[0]],
                tok_recv.at[zz * 4 + xx, c, h], seq=target,
            )
        )
        count[0] += 1

    def wait_half(zz, xx, cc, h):
        pltpu.make_async_copy(
            half(zz, xx, cc, h), half(zz, xx, cc, h), tok_recv.at[zz * 4 + xx, cc, h]
        ).wait()

    def wait_first():
        for i, source in ((0, down), (1, up), (2, across)):
            pltpu.make_async_copy(
                tok.at[here, c, source], tok.at[here, c, source], tok_first.at[i]
            ).wait()
        local_first.wait()

    def spread(zz):
        for a, b in ((0, 1), (1, 0)):
            send_half(zz, x, a, x_right)
            send_half(zz, x, b, x_left)

    def relay(zz):
        wait_half(zz, left, c, 0)
        send_half(zz, left, 0, x_right)
        wait_half(zz, right, c, 1)
        send_half(zz, right, 1, x_left)

    def share(zz, xx, h):
        send_half(zz, xx, h, sibling)

    def slot(yy, cc, i):
        return (yy * 2 + cc) * GROUPS + i

    def send_group(i):
        mine = cols.at[slot(y, c, i)]
        for n, (kind, target) in enumerate(
            ((0, seq_of(z, x, up, 0)), (1, seq_of(z, x, up, 1)), (0, seq_of(z, x, down, 0)), (1, seq_of(z, x, down, 1)))
        ):
            launch(
                remote(own.at[kind, i], mine, col_send.at[i * 5 + n], col_recv.at[slot(y, c, i)], seq=target)
            )
        launch(
            remote(
                own.at[1 - c, i], mine, col_send.at[i * 5 + 4], col_recv.at[slot(y, c, i)], seq=sibling
            )
        )
        pltpu.make_async_copy(own.at[c, i], mine, col_recv.at[slot(y, c, i)]).start()

    def wait_col(at):
        pltpu.make_async_copy(cols.at[at], cols.at[at], col_recv.at[at]).wait()

    forwarded = [0]

    def relay_group(i):
        source, target = (down, up) if i % 2 == 0 else (up, down)
        for cc in range(2):
            at = slot(source, cc, i)
            wait_col(at)
            launch(
                remote(
                    cols.at[at], cols.at[at], col_send.at[5 * GROUPS + forwarded[0]], col_recv.at[at],
                    seq=seq_of(z, x, target, c),
                )
            )
            forwarded[0] += 1

    def compute_group(i):
        conv_group(i * GROUP, g_ref, k_ref, v_ref, f_ref, fg_all, key_rows, value_rows, tables)
        own[0, i] = key_rows[...].reshape(HALF, GROUP, RADIX).astype(BF16)
        own[1, i] = value_rows[...].reshape(HALF, GROUP, RADIX).astype(BF16)

    compute_group(0)
    send_group(0)
    wait_first()
    spread(z)
    for h in range(2):
        send_half(z, x, h, z_other)
        share(z, x, h)
    compute_group(1)
    send_group(1)
    compute_group(2)
    send_group(2)
    relay(z)
    for h in range(2):
        wait_half(1 - z, x, c, h)
    spread(1 - z)
    relay_group(0)
    compute_group(3)
    send_group(3)
    fg_copy = remote(
        fg_all.at[:, pl.ds((1 - dp) * 32, 32)], fg_in, fg_sem.at[0], fg_sem.at[1], dp=1 - dp
    )
    launch(fg_copy)
    relay_group(1)
    for h in range(2):
        share(1 - z, x, h)
    for xx, h in ((left, 0), (right, 1)):
        share(z, xx, h)
    for xx, h in ((left, 1), (right, 0)):
        wait_half(z, xx, c, h)
        share(z, xx, h)
    for h in range(2):
        wait_half(z, far, c, h)
        share(z, far, h)
    relay_group(2)
    relay(1 - z)
    relay_group(3)
    for xx, h in ((left, 0), (right, 1)):
        share(1 - z, xx, h)
    for xx, h in ((left, 1), (right, 0)):
        wait_half(1 - z, xx, c, h)
        share(1 - z, xx, h)
    for h in range(2):
        wait_half(1 - z, far, c, h)
        share(1 - z, far, h)
    fg_copy.wait_recv()
    fg_ref[...] = fg_all[:, pl.ds(dp * 32, 32)] + fg_in[...]
    for i in range(GROUPS):
        wait_col(slot(y, 0, i))
        wait_col(slot(y, 1, i))
        wait_col(slot(across, 0, i))
        wait_col(slot(across, 1, i))
        source = up if i % 2 == 0 else down
        wait_col(slot(source, 0, i))
        wait_col(slot(source, 1, i))

    def multiply(zx, fresh):
        left_side = jnp.concatenate(
            [
                cols[:, zx * 8 + yy * 2 + cc].reshape(PIECES * GROUP, RADIX)
                for cc in range(2)
                for yy in range(4)
            ],
            axis=1,
        )

        def tile(n, carry):
            j, at = n // 2, pl.multiple_of(n % 2 * 256, 256)
            right_side = tok[zx, :, :, :, pl.ds(pl.multiple_of(n * 256, 256), 256)].reshape(1024, 256)
            term = dot(left_side, right_side)
            if fresh:
                part_ref[j, :, pl.ds(at, 256)] = term
            else:
                part_ref[j, :, pl.ds(at, 256)] += term
            return carry

        lax.fori_loop(0, 4, tile, 0)

    for h in range(2):
        wait_half(z, x, 1 - c, h)
    multiply(here, True)

    for zz, xx in ((z, left), (z, right), (z, far), (1 - z, x), (1 - z, left), (1 - z, right), (1 - z, far)):
        for h in range(2):
            wait_half(zz, xx, 1 - c, h)

    def rest(i, carry):
        multiply((here + i) % 8, False)
        return carry

    lax.fori_loop(1, 8, rest, 0)
    for copy in pending:
        copy.wait_send()


def gradient_parts(g, k, v, f, tokens):
    tabs = [jnp.asarray(t) for t in fourier_tables()]
    vm = pl.BlockSpec(memory_space=pltpu.VMEM)
    dma = pltpu.SemaphoreType.DMA
    return pl.pallas_call(
        gradient_kernel,
        out_shape=(
            jax.ShapeDtypeStruct((2, 512, 512), F32),
            jax.ShapeDtypeStruct((64, HALF // 2, RADIX), F32),
        ),
        in_specs=[vm] * 10,
        out_specs=[vm] * 2,
        scratch_shapes=[
            pltpu.VMEM((8, 2, 4, RADIX, 1024), BF16),
            pltpu.VMEM((PIECES, HALF, GROUP, RADIX), BF16),
            pltpu.VMEM((2, GROUPS, HALF, GROUP, RADIX), BF16),
            pltpu.VMEM((64, HALF, RADIX), F32),
            pltpu.VMEM((64, HALF // 2, RADIX), F32),
            pltpu.VMEM((HALF * GROUP, RADIX), F32),
            pltpu.VMEM((HALF * GROUP, RADIX), F32),
            dma((4,)), dma((3,)), dma((8, 2, 2)), dma((32,)), dma((PIECES,)), dma((28,)), dma((2,)),
        ],
        compiler_params=pltpu.CompilerParams(
            collective_id=0, has_side_effects=True, vmem_limit_bytes=56 << 20
        ),
        name="gradient_parts",
    )(g, k, v, f, tokens, *tabs)


def product(left, right):
    left_high, left_low = parts(left)
    right_high, right_low = parts(right)
    left_side = jnp.concatenate([left_high, left_low, left_high], axis=1)
    right_side = jnp.concatenate([right_high, right_high, right_low], axis=0)
    return dot(left_side, right_side)


def newton_kernel(part_ref, update_ref, landed, gram, gram_in, current, send, recv, gram_sem):
    z, x, y, c = place()
    dp = lax.axis_index("dp")
    me = lax.axis_index("seq")
    targets = [
        (seq_of(y // 2, 2 * (y % 2) + j, 2 * c + z, x // 2), x % 2) for j in range(2)
    ]
    source_y, source_c, source_z = 2 * z + x // 2, y // 2, y % 2
    sources = [(seq_of(source_z, 2 * c + dp, source_y, source_c), d) for d in range(2)]
    barrier = pltpu.get_barrier_semaphore()
    expected = jnp.int32(1)
    for seq, d in sources:
        other = jnp.logical_or(seq != me, d != dp)

        @pl.when(other)
        def _():
            pl.semaphore_signal(
                barrier, inc=1, device_id={"seq": seq, "dp": d}, device_id_type=pl.DeviceIdType.MESH
            )

    for seq, d in targets:
        expected = expected + jnp.logical_or(seq != me, d != dp).astype(jnp.int32)
    pl.semaphore_signal(barrier, inc=1, device_id={"dp": 1 - dp}, device_id_type=pl.DeviceIdType.MESH)
    pl.semaphore_wait(barrier, expected)

    for j, (seq, d) in enumerate(targets):
        other = jnp.logical_or(seq != me, d != dp)
        copy = remote(part_ref.at[j], landed.at[dp], send.at[j], recv.at[dp], seq=seq, dp=d)

        @pl.when(other)
        def _():
            copy.start()

        @pl.when(jnp.logical_not(other))
        def _():
            pltpu.make_async_copy(part_ref.at[j], landed.at[dp], recv.at[dp]).start()

    for d in range(2):
        pltpu.make_async_copy(landed.at[d], landed.at[d], recv.at[d]).wait()
    columns = landed[0] + landed[1]
    current[...] = columns.T
    gram[...] = product(current[...], columns)
    exchange = remote(gram, gram_in, gram_sem.at[0], gram_sem.at[1], dp=1 - dp)
    exchange.start()
    exchange.wait()
    raw = gram[...] + gram_in[...]
    diagonal = lax.broadcasted_iota(jnp.int32, raw.shape, 0) == lax.broadcasted_iota(
        jnp.int32, raw.shape, 1
    )
    norm = jnp.sqrt(jnp.sum(jnp.where(diagonal, raw, 0.0), keepdims=True)) + 1e-07
    scale = 1.0 / norm
    gram_in[...] = raw * scale * scale
    current[...] = current[...] * scale

    def step(i, carry):
        gram_now = gram_in[...]
        mixer = COEF_B * gram_now + COEF_C * product(gram_now, gram_now)
        current[...] = COEF_A * current[...] + product(mixer, current[...])
        half = COEF_A * gram_now + product(mixer, gram_now)
        gram_in[...] = COEF_A * half + product(half, mixer)
        return carry

    lax.fori_loop(0, NS_STEPS - 1, step, 0)
    gram_now = gram_in[...]
    mixer = COEF_B * gram_now + COEF_C * product(gram_now, gram_now)
    update_ref[...] = (COEF_A * current[...] + product(mixer, current[...])) * 32.0
    for j, (seq, d) in enumerate(targets):
        other = jnp.logical_or(seq != me, d != dp)
        copy = remote(part_ref.at[j], landed.at[dp], send.at[j], recv.at[dp], seq=seq, dp=d)

        @pl.when(other)
        def _():
            copy.wait_send()


def newton(part):
    vm = pl.BlockSpec(memory_space=pltpu.VMEM)
    dma = pltpu.SemaphoreType.DMA
    return pl.pallas_call(
        newton_kernel,
        out_shape=jax.ShapeDtypeStruct((512, 512), F32),
        in_specs=[vm],
        out_specs=vm,
        scratch_shapes=[
            pltpu.VMEM((2, 512, 512), F32),
            pltpu.VMEM((512, 512), F32),
            pltpu.VMEM((512, 512), F32),
            pltpu.VMEM((512, 512), F32),
            dma((2,)), dma((2,)), dma((2,)),
        ],
        compiler_params=pltpu.CompilerParams(
            collective_id=1, has_side_effects=True, vmem_limit_bytes=48 << 20
        ),
        name="newton",
    )(part)


def quarters(tokens):
    blocks = tokens.reshape(RADIX, 8, 512)
    return jnp.stack([jnp.concatenate([blocks[:, 2 * y], blocks[:, 2 * y + 1]], axis=1) for y in range(4)])


def body(tokens, queries, keys, values, upstream, filters):
    conv_grad = (upstream[0].astype(F32) * queries[0].astype(F32)).astype(BF16)
    sent = jnp.stack([item.T.reshape(64, 64, RADIX) for item in (conv_grad, keys[0], values[0])], axis=1)
    landed = lax.all_to_all(sent, "seq", split_axis=0, concat_axis=0, tiled=True)
    g, k, v = (landed[:, i].transpose(1, 0, 2) for i in range(3))
    f = filters.T.reshape(64, HALF, RADIX)
    part, filter_half = gradient_parts(g, k, v, f, quarters(tokens[0]))
    update = newton(part)
    filter_grad = filter_half.reshape(64, HALF // 2 * RADIX).T
    return (update[None], filter_grad)


def solution(mesh):
    return jax.shard_map(
        body,
        mesh=mesh,
        in_specs=(
            P("dp", "seq", None),
            P("dp", "seq", None),
            P("dp", "seq", None),
            P("dp", "seq", None),
            P("dp", "seq", None),
            P(None, "seq"),
        ),
        out_specs=(P("seq", None, "dp"), P("dp", "seq")),
        check_vma=False,
    )
```

time: 936 us -> 269 us (0.29); the launches traced: 925 us -> 268 us
  waiting for transfers between devices: 382 us -> 20.5 us
  matrix products: 237 us -> 0 us
  blocking collectives: 226 us -> 0 us
  Pallas kernels: 0 us -> 198 us
  starting transfers between devices: 34 us -> 10.4 us
  local copies, waits for them, and re-layouts: 22.1 us -> 37.1 us
  between operations: 15.6 us -> 0.82 us
    dot_general x46 -> x0, matrix products: 237 us -> none  [the longest x30 180 us: contract(): return jnp.einsum(form, left, right, precision=lax.Precision.HIGHEST)]
    all_to_all x1 -> x0, blocking collectives: 220 us -> none  [body(): lax.all_to_all(grad_rep, 'seq', split_axis=0, concat_axis=1, tiled=True)]
    pallas_call x0 -> x2, Pallas kernels: none -> 198 us  [the longest x1 109 us: gradient_parts(): pl.pallas_call(gradient_kernel, out_shape=(jax.ShapeDtypeStruct((2, 512,...]
    psum x5 -> x0, waiting for transfers between devices: 193 us -> none  [body(): gram = lax.psum(row_products(current), 'dp')]
    all_to_all x4 -> x1, waiting for transfers between devices: 124 us -> 20.5 us  [body(): lax.all_to_all(sent, 'seq', split_axis=0, concat_axis=0, tiled=True)]
    reduce_scatter x2 -> x0, waiting for transfers between devices: 65.6 us -> none  [the longest x1 34.8 us: body(): lax.psum_scatter(partial_block, 'dp', scatter_dimension=1, tiled=True)]
    all_to_all x4 -> x1, starting transfers between devices: 33.1 us -> 10.4 us  [body(): lax.all_to_all(sent, 'seq', split_axis=0, concat_axis=0, tiled=True)]
    unnamed x42 -> x41, local copies, waits for them, and re-layouts: 13.4 us -> 29.3 us
  transfers between devices with their start and end apart: 11 -> 1, of which waited for: 10 -> 1; matrix products, arithmetic and copies ran while one was open for 12% -> 7% of each run, Pallas kernels for 0% -> 0%
where the time goes in v2:
time: 269 us; the launch traced here: 268 us
  Pallas kernels  198 us (74%)
  local copies, waits for them, and re-layouts  37.1 us (14%)
  waiting for transfers between devices  20.5 us (8%)
  starting transfers between devices  10.4 us (4%)
    pallas_call x1, Pallas kernels, gradient_parts(): pl.pallas_call(gradient_kernel, out_shape=(jax.ShapeDtypeStruct((2, 512,...  109 us
    pallas_call x1, Pallas kernels, newton(): pl.pallas_call(newton_kernel, out_shape=jax.ShapeDtypeStruct((512, 512),...  88.6 us
    unnamed x41, local copies, waits for them, and re-layouts  29.3 us
    all_to_all x1, waiting for transfers between devices, body(): lax.all_to_all(sent, 'seq', split_axis=0, concat_axis=0, tiled=True)  20.5 us
    all_to_all x1, starting transfers between devices, body(): lax.all_to_all(sent, 'seq', split_axis=0, concat_axis=0, tiled=True)  10.4 us
  transfers between devices with their start and end apart: 1, of which 1 were waited for; matrix products, arithmetic and copies ran while one was open for 7% of the time, Pallas kernels for 0%

profile of v2, /device:TPU:1, one launch (start us, length us, event | category | flops | bytes accessed | tf_op | source)
XLA Modules:
  0.0 268.4 jit_solution(6154061025529770093)
XLA Ops:
  0.6 1.7 copy.30
  2.4 1.6 copy.31
  4.0 1.3 copy.32
  5.3 1.6 copy.29
  6.9 0.3 multiply_convert_fusion
  7.2 0.9 copy-done.1
  8.1 0.3 pad_maximum_fusion
  8.5 2.3 copy.33
  10.8 10.4 %all-to-all-start = ((bf16[64,3,64,128]{3,2,1,0:T(8,128)(2,1)}), bf16[64,3,64,128]{3,2,1,0:T(8,128)(2,1)S(1)}, u32[]{:S(2)}, u32[]{:S(2)}) async-start(bf16[64,3,64,128]{3,2,1,0:T(8,128)(2,1)} %copy.33), calls=%async_computation | async-start | bytes 6291456 | tf_op jit(solution)/shard_map/all_to_all | solution.py:531
  21.2 2.3 copy.37
  23.4 2.1 fusion.1
  25.6 1.7 copy.49
  27.2 1.7 copy.55
  28.9 1.7 copy.54
  30.5 1.7 copy.53
  32.2 1.7 copy.52
  33.9 0.8 copy.51
  34.6 0.8 copy.50
  35.4 0.8 copy.56
  36.2 3.4 %copy.57 = f32[8,8,64,128]{3,2,1,0:T(8,128)} copy(f32[8,8,64,128]{3,1,2,0:T(8,128)} %bitcast.63) | data formatting | bytes 4194304
  39.6 0.1 maximum_bitcast_fusion
  39.7 0.1 maximum_bitcast_fusion.2
  39.8 1.1 pad_maximum_fusion.1.tok_ref
  40.9 20.5 %all-to-all-done = bf16[64,3,64,128]{3,2,1,0:T(8,128)(2,1)S(1)} async-done(((bf16[64,3,64,128]{3,2,1,0:T(8,128)(2,1)}), bf16[64,3,64,128]{3,2,1,0:T(8,128)(2,1)S(1)}, u32[]{:S(2)}, u32[]{:S(2)}) %all-to-all-start) | async-done | bytes 3145760 | tf_op jit(solution)/shard_map/all_to_all | solution.py:531
  61.4 0.7 fusion
  62.1 1.6 copy.64
  63.7 2.7 copy_bitcast_fusion
  66.4 109.3 %gradient_parts.1 = (f32[2,512,512]{2,1,0:T(8,128)}, f32[64,32,128]{2,1,0:T(8,128)}) custom-call(bf16[64,64,128]{2,1,0:T(8,128)(2,1)} %bitcast.58, bf16[64,64,128]{2,1,0:T(8,128)(2,1)} %get-tuple-element.18.k_ref, bf16[64,64,128]{2,1,0:T(8,128)(2,1)} %get-tuple-element.17.v_ref, f32[64,64,128]{2,1,0:T(8,128)} %bitcast.57, ...), custom_call_target="tpu_custom_call" | custom-call | tf_op jit(solution)/shard_map/gradient_parts/pallas_call | solution.py:393
  175.7 1.6 copy-done
  177.3 88.6 %newton.1 = f32[512,512]{1,0:T(8,128)S(1)} custom-call(f32[2,512,512]{2,1,0:T(8,128)S(1)} %copy-done), custom_call_target="tpu_custom_call" | custom-call | tf_op jit(solution)/shard_map/newton/pallas_call | solution.py:504
  265.9 1.6 copy.63
  267.4 1.0 copy.66
  (22 shorter events, 0.0 us)
Async XLA Ops:
  0.6 3.3 %copy-start.2 = (bf16[1,128,4096]{2,1,0:T(8,128)(2,1)S(1)}, bf16[1,128,4096]{2,1,0:T(8,128)(2,1)}, u32[]{:S(2)}) copy-start(bf16[1,128,4096]{2,1,0:T(8,128)(2,1)} %param.14) | copy-start | bytes 3145732
  6.9 1.2 copy-start.1
  10.8 50.6 %all-to-all-start = ((bf16[64,3,64,128]{3,2,1,0:T(8,128)(2,1)}), bf16[64,3,64,128]{3,2,1,0:T(8,128)(2,1)S(1)}, u32[]{:S(2)}, u32[]{:S(2)}) async-start(bf16[64,3,64,128]{3,2,1,0:T(8,128)(2,1)} %copy.33), calls=%async_computation | async-start | bytes 6291456 | tf_op jit(solution)/shard_map/all_to_all | solution.py:531
  34.6 5.1 %copy-start.4 = (bf16[128,1,512]{2,0,1:T(8,128)(2,1)S(1)}, bf16[128,1,512]{2,0,1:T(8,128)(2,1)}, u32[]{:S(2)}) copy-start(bf16[128,1,512]{2,0,1:T(8,128)(2,1)} %copy.55) | copy-start | bytes 393220
  35.4 4.3 %copy-start.5 = (bf16[128,1,512]{2,0,1:T(8,128)(2,1)S(1)}, bf16[128,1,512]{2,0,1:T(8,128)(2,1)}, u32[]{:S(2)}) copy-start(bf16[128,1,512]{2,0,1:T(8,128)(2,1)} %copy.54) | copy-start | bytes 393220
  36.2 3.4 %copy-start.7 = (bf16[128,1,512]{2,0,1:T(8,128)(2,1)S(1)}, bf16[128,1,512]{2,0,1:T(8,128)(2,1)}, u32[]{:S(2)}) copy-start(bf16[128,1,512]{2,0,1:T(8,128)(2,1)} %copy.49) | copy-start | bytes 393220
  36.2 3.4 %copy-start.9 = (bf16[128,1,512]{2,0,1:T(8,128)(2,1)S(1)}, bf16[128,1,512]{2,0,1:T(8,128)(2,1)}, u32[]{:S(2)}) copy-start(bf16[128,1,512]{2,0,1:T(8,128)(2,1)} %copy.52) | copy-start | bytes 393220
  36.2 3.4 %copy-start.10 = (bf16[128,1,512]{2,0,1:T(8,128)(2,1)S(1)}, bf16[128,1,512]{2,0,1:T(8,128)(2,1)}, u32[]{:S(2)}) copy-start(bf16[128,1,512]{2,0,1:T(8,128)(2,1)} %copy.51) | copy-start | bytes 393220
  36.2 3.4 %copy-start.11 = (bf16[128,1,512]{2,0,1:T(8,128)(2,1)S(1)}, bf16[128,1,512]{2,0,1:T(8,128)(2,1)}, u32[]{:S(2)}) copy-start(bf16[128,1,512]{2,0,1:T(8,128)(2,1)} %copy.50) | copy-start | bytes 393220
  36.2 3.5 %copy-start.6 = (bf16[128,1,512]{2,0,1:T(8,128)(2,1)S(1)}, bf16[128,1,512]{2,0,1:T(8,128)(2,1)}, u32[]{:S(2)}) copy-start(bf16[128,1,512]{2,0,1:T(8,128)(2,1)} %copy.53) | copy-start | bytes 393220
  36.2 3.5 %copy-start.8 = (bf16[128,1,512]{2,0,1:T(8,128)(2,1)S(1)}, bf16[128,1,512]{2,0,1:T(8,128)(2,1)}, u32[]{:S(2)}) copy-start(bf16[128,1,512]{2,0,1:T(8,128)(2,1)} %copy.56) | copy-start | bytes 393220
  175.7 1.6 copy-start
  177.3 88.6 %copy-start.3 = (f32[64,32,128]{2,1,0:T(8,128)S(1)}, f32[64,32,128]{2,1,0:T(8,128)}, u32[]{:S(2)}) copy-start(f32[64,32,128]{2,1,0:T(8,128)} %get-tuple-element.5) | copy-start | bytes 3145732

commit v3 on v2

v3 whole, which is shorter than its diff:
```python
import math

import jax
import jax.numpy as jnp
import numpy as np
from jax import lax
from jax.experimental import pallas as pl
from jax.experimental.pallas import tpu as pltpu
from jax.sharding import PartitionSpec as P

F32, BF16 = jnp.float32, jnp.bfloat16
RADIX = 128
HALF = 64
NS_STEPS = 5
COEF_A = 3.4445
COEF_B = -4.775
COEF_C = 2.0315
ROWS = 72


def split_table(table):
    high = np.asarray(table, np.float32).astype(jnp.bfloat16)
    low = (np.asarray(table, np.float64) - high.astype(np.float64)).astype(jnp.bfloat16)
    return high, low


def fourier_tables():
    total = RADIX * RADIX
    spot = np.arange(RADIX)
    used = np.arange(HALF + 1)
    outer = 2.0 * math.pi * (np.outer(used, np.arange(HALF)) % RADIX) / RADIX
    first = np.zeros((2 * ROWS, HALF))
    first[: HALF + 1] = np.cos(outer)
    first[ROWS : ROWS + HALF + 1] = -np.sin(outer)
    weight = np.where((used == 0) | (used == HALF), 1.0, 2.0)[:, None] / total
    last = np.zeros((2 * ROWS, HALF))
    last[: HALF + 1] = np.cos(outer) * weight
    last[ROWS : ROWS + HALF + 1] = -np.sin(outer) * weight
    last = last.T
    inner = 2.0 * math.pi * (np.outer(spot, spot) % RADIX) / RADIX
    real, imag = np.cos(inner), -np.sin(inner)
    forward = np.block([[real, imag], [-imag, real]])
    turn = 2.0 * math.pi * np.outer(used, spot) / total
    twist = np.zeros((2, ROWS, RADIX), np.float32)
    twist[0, : HALF + 1] = np.cos(turn)
    twist[1, : HALF + 1] = -np.sin(turn)
    first_high, first_low = split_table(first)
    last_high, last_low = split_table(last)
    ahead_high, ahead_low = split_table(forward)
    back_high, back_low = split_table(forward.T)
    return (
        np.concatenate([first_high, first_low, first_high], 1),
        np.concatenate([ahead_high, ahead_high, ahead_low], 0),
        np.concatenate([back_high, back_high, back_low], 0),
        np.concatenate([last_high, last_low, last_high], 1),
        twist,
    )


def dot(left, right):
    return jnp.dot(left, right, preferred_element_type=F32)


def parts(value):
    high = value.astype(BF16)
    return high, (value - high.astype(F32)).astype(BF16)


def convolve_pair(grads, inputs, filters, tables):
    first_ref, ahead_ref, back_ref, last_ref, twist_ref = tables
    turn_real, turn_imag = twist_ref[0], twist_ref[1]
    signals = jnp.concatenate([grads[0], inputs[0], grads[1], inputs[1]], axis=1)
    signals = jnp.concatenate([signals, signals], axis=0)
    spread = dot(first_ref[:, : 2 * HALF], signals)
    high, low = parts(jnp.concatenate(filters, axis=1))
    spread_filter = dot(first_ref[...], jnp.concatenate([high, high, low], axis=0))
    turned = []
    for block in (spread, spread_filter):
        for at in range(0, block.shape[1], RADIX):
            real, imag = block[:ROWS, at : at + RADIX], block[ROWS:, at : at + RADIX]
            turned.append(
                jnp.concatenate(
                    [real * turn_real - imag * turn_imag, real * turn_imag + imag * turn_real], axis=1
                )
            )
    high, low = parts(jnp.concatenate(turned, axis=0))
    spectra = dot(jnp.concatenate([high, low, high], axis=1), ahead_ref[...])
    spec = [
        (spectra[i * ROWS : (i + 1) * ROWS, :RADIX], spectra[i * ROWS : (i + 1) * ROWS, RADIX:])
        for i in range(6)
    ]
    products = []
    for which in range(2):
        grad_real, grad_imag = spec[2 * which]
        input_real, input_imag = spec[2 * which + 1]
        filter_real, filter_imag = spec[4 + which]
        for other_real, other_imag, flip in (
            (filter_real, filter_imag, 0),
            (input_real, input_imag, 0),
        ):
            products.append(
                jnp.concatenate(
                    [
                        grad_real * other_real + grad_imag * other_imag,
                        grad_imag * other_real - grad_real * other_imag,
                    ],
                    axis=1,
                )
            )
    high, low = parts(jnp.concatenate(products, axis=0))
    mixed = dot(jnp.concatenate([high, low, high], axis=1), back_ref[...])
    columns = []
    for i in range(4):
        real, imag = mixed[i * ROWS : (i + 1) * ROWS, :RADIX], mixed[i * ROWS : (i + 1) * ROWS, RADIX:]
        columns.append(
            jnp.concatenate(
                [real * turn_real + imag * turn_imag, imag * turn_real - real * turn_imag], axis=0
            )
        )
    high, low = parts(jnp.concatenate(columns, axis=1))
    result = dot(last_ref[...], jnp.concatenate([high, high, low], axis=0))
    return [result[:, i * RADIX : (i + 1) * RADIX] for i in range(4)]


GROUP = 16


GROUPS = 4


def conv_group(at, in_rows, f_ref, fg_ref, out_rows, tables):
    def pair(j, carry):
        chans = [at + 2 * j, at + 2 * j + 1]
        spots = [pl.ds(2 * j + i, HALF, stride=GROUP) for i in range(2)]
        keys = [in_rows[1, spot, :] for spot in spots]
        values = [in_rows[2, spot, :] for spot in spots]
        inputs = [(a * b).astype(BF16) for a, b in zip(keys, values)]
        grads = [in_rows[0, spot, :].astype(BF16) for spot in spots]
        out = convolve_pair(grads, inputs, [f_ref[chan] for chan in chans], tables)
        for i in range(2):
            back = out[2 * i].astype(BF16).astype(F32)
            fg_ref[chans[i]] = out[2 * i + 1]
            out_rows[0, spots[i], :] = back * values[i]
            out_rows[1, spots[i], :] = back * keys[i]
        return carry

    lax.fori_loop(0, GROUP // 2, pair, 0)


def place():
    me = lax.axis_index("seq")
    return me // 32, me // 8 % 4, me // 2 % 4, me % 2


def seq_of(z, x, y, c):
    return ((z * 4 + x) * 4 + y) * 2 + c


MESH = pl.DeviceIdType.MESH


def remote(src, dst, send, recv, **device):
    return pltpu.make_async_remote_copy(
        src_ref=src, dst_ref=dst, send_sem=send, recv_sem=recv, device_id=device, device_id_type=MESH
    )


def wait_bytes(ref, sem):
    pltpu.make_async_copy(ref, ref, sem).wait()


def product(left, right):
    left_high, left_low = parts(left)
    right_high, right_low = parts(right)
    left_side = jnp.concatenate([left_high, left_low, left_high], axis=1)
    right_side = jnp.concatenate([right_high, right_high, right_low], axis=0)
    return dot(left_side, right_side)


def gradient_kernel(
    sent, f_ref, tok_ref, t0, t1, t2, t3, t4,
    update_ref, fg_ref,
    got, tok, cols, own, fg_all, fg_in, in_rows, out_rows, part, landed, gram, gram_in, current,
    swap_send, swap_recv, swap_own, tok_first, tok_first_send, tok_recv, tok_send, col_recv, col_send,
    fg_sem, part_send, part_recv, gram_send, gram_recv,
):
    tables = (t0, t1, t2, t3, t4)
    z, x, y, c = place()
    me = lax.axis_index("seq")
    dp = lax.axis_index("dp")
    n_seq = lax.axis_size("seq")
    up, down, across = (y + 1) % 4, (y + 3) % 4, (y + 2) % 4
    right, left, far = (x + 1) % 4, (x + 3) % 4, (x + 2) % 4
    sibling = seq_of(z, x, y, 1 - c)
    x_right, x_left = seq_of(z, right, y, c), seq_of(z, left, y, c)
    z_other = seq_of(1 - z, x, y, c)
    targets = [seq_of(j, (y + 2 * j) % 4, 2 * c + z, x // 2) for j in range(2)]
    owner_dp = x % 2
    source = seq_of(y % 2, 2 * c + dp, (x + 2 * z) % 4, y // 2)

    barrier = pltpu.get_barrier_semaphore()

    def greet(d, carry):
        pl.semaphore_signal(barrier, inc=1, device_id={"seq": (me + d) % n_seq}, device_id_type=MESH)
        return carry

    lax.fori_loop(1, n_seq, greet, 0)
    pl.semaphore_signal(barrier, inc=1, device_id={"dp": 1 - dp}, device_id_type=MESH)
    pl.semaphore_signal(barrier, inc=1, device_id={"seq": source, "dp": 1 - dp}, device_id_type=MESH)
    pl.semaphore_wait(barrier, n_seq + 2 * ((x + dp) % 2))

    def swap(d, carry):
        peer = (me + d) % n_seq
        remote(sent.at[peer], got.at[me], swap_send, swap_recv, seq=peer).start()
        return carry

    lax.fori_loop(1, n_seq, swap, 0)
    swap_here = pltpu.make_async_copy(sent.at[me], got.at[me], swap_own)
    swap_here.start()

    pending = []

    def launch(copy):
        copy.start()
        pending.append(copy)

    here = z * 4 + x
    for i, target in enumerate((up, down, across)):
        launch(
            remote(
                tok_ref.at[target], tok.at[here, c, y], tok_first_send.at[i], tok_first.at[i],
                seq=seq_of(z, x, target, c),
            )
        )
    local_first = pltpu.make_async_copy(tok_ref.at[y], tok.at[here, c, y], tok_first.at[3])
    local_first.start()

    count = [0]

    def half(zz, xx, cc, h):
        return tok.at[zz * 4 + xx, cc, pl.ds(2 * h, 2)]

    def send_half(zz, xx, h, target):
        launch(
            remote(
                half(zz, xx, c, h), half(zz, xx, c, h), tok_send.at[count[0]],
                tok_recv.at[zz * 4 + xx, c, h], seq=target,
            )
        )
        count[0] += 1

    def wait_half(zz, xx, cc, h):
        wait_bytes(half(zz, xx, cc, h), tok_recv.at[zz * 4 + xx, cc, h])

    def wait_first():
        for i, source_y in ((0, down), (1, up), (2, across)):
            wait_bytes(tok.at[here, c, source_y], tok_first.at[i])
        local_first.wait()

    def spread(zz):
        for a, b in ((0, 1), (1, 0)):
            send_half(zz, x, a, x_right)
            send_half(zz, x, b, x_left)

    def relay(zz):
        wait_half(zz, left, c, 0)
        send_half(zz, left, 0, x_right)
        wait_half(zz, right, c, 1)
        send_half(zz, right, 1, x_left)

    def share(zz, xx, h):
        send_half(zz, xx, h, sibling)

    def slot(yy, cc, i):
        return (yy * 2 + cc, i)

    def send_group(i):
        mine = cols.at[slot(y, c, i)]
        arrival = col_recv.at[slot(y, c, i)]
        for n, (kind, target) in enumerate(((0, up), (1, up), (0, down), (1, down))):
            launch(
                remote(own.at[kind, i], mine, col_send.at[i * 5 + n], arrival, seq=seq_of(z, x, target, kind))
            )
        launch(remote(own.at[1 - c, i], mine, col_send.at[i * 5 + 4], arrival, seq=sibling))
        pltpu.make_async_copy(own.at[c, i], mine, arrival).start()

    def wait_col(at):
        wait_bytes(cols.at[at], col_recv.at[at])

    forwarded = [0]

    def relay_group(i):
        source_y, target = (down, up) if i % 2 == 0 else (up, down)
        for cc in range(2):
            at = slot(source_y, cc, i)
            wait_col(at)
            launch(
                remote(
                    cols.at[at], cols.at[at], col_send.at[5 * GROUPS + forwarded[0]], col_recv.at[at],
                    seq=seq_of(z, x, target, c),
                )
            )
            forwarded[0] += 1

    def compute_group(i):
        for kind in range(3):
            in_rows[kind] = got[:, kind, GROUP * i : GROUP * (i + 1), :].astype(F32).reshape(HALF * GROUP, RADIX)
        conv_group(i * GROUP, in_rows, f_ref, fg_all, out_rows, tables)
        for kind in range(2):
            own[kind, i] = out_rows[kind].reshape(HALF, GROUP, RADIX).astype(BF16)

    wait_bytes(got.at[pl.ds(0, 63)], swap_recv)
    swap_here.wait()
    wait_first()
    spread(z)
    for h in range(2):
        send_half(z, x, h, z_other)
        share(z, x, h)
    compute_group(0)
    send_group(0)
    relay(z)
    compute_group(1)
    send_group(1)
    for h in range(2):
        wait_half(1 - z, x, c, h)
    spread(1 - z)
    relay_group(0)
    for xx, h in ((left, 0), (right, 1)):
        share(z, xx, h)
    compute_group(2)
    send_group(2)
    relay_group(1)
    for h in range(2):
        share(1 - z, x, h)
    compute_group(3)
    send_group(3)
    fg_copy = remote(
        fg_all.at[:, pl.ds((1 - dp) * 32, 32)], fg_in, fg_sem.at[0], fg_sem.at[1], dp=1 - dp
    )
    launch(fg_copy)
    relay(1 - z)
    relay_group(2)
    for xx, h in ((left, 1), (right, 0)):
        wait_half(z, xx, c, h)
        share(z, xx, h)
    for h in range(2):
        wait_half(z, far, c, h)
        share(z, far, h)
    for xx, h in ((left, 0), (right, 1)):
        share(1 - z, xx, h)
    for xx, h in ((left, 1), (right, 0)):
        wait_half(1 - z, xx, c, h)
        share(1 - z, xx, h)
    relay_group(3)
    for h in range(2):
        wait_half(1 - z, far, c, h)
        share(1 - z, far, h)

    def wait_group(i):
        for cc in range(2):
            wait_col(slot(y, cc, i))
            wait_col(slot(across, cc, i))
            wait_col(slot(up if i % 2 == 0 else down, cc, i))

    def multiply(zx, side, fresh):
        left_side = jnp.concatenate(
            [
                cols[:, pl.ds(2 * side, 2), zx * 8 + yy * 2 + cc].reshape(256, RADIX)
                for cc in range(2)
                for yy in range(4)
            ],
            axis=1,
        )

        def tile(n, carry):
            j, at = n // 2, pl.multiple_of(n % 2 * 256, 256)
            right_side = tok[zx, :, :, :, pl.ds(pl.multiple_of(n * 256, 256), 256)].reshape(1024, 256)
            term = dot(left_side, right_side).reshape(8, 32, 256)
            if fresh:
                part[j, :, pl.ds(32 * side, 32), pl.ds(at, 256)] = term
            else:
                part[j, :, pl.ds(32 * side, 32), pl.ds(at, 256)] += term
            return carry

        lax.fori_loop(0, 4, tile, 0)

    stays = [jnp.logical_and(target == me, owner_dp == dp) for target in targets]

    def part_copy(j, side):
        view = (slice(None), pl.ds(32 * side, 32))
        src, dst = part.at[(j, *view)], landed.at[(dp, *view)]
        arrival = part_recv.at[dp, side]
        away = remote(src, dst, part_send.at[j, side], arrival, seq=targets[j], dp=owner_dp)
        return away, pltpu.make_async_copy(src, dst, arrival)

    def send_parts(side):
        for j in range(2):
            away, at_home = part_copy(j, side)

            @pl.when(stays[j])
            def _():
                at_home.start()

            @pl.when(jnp.logical_not(stays[j]))
            def _():
                away.start()

    def rest(side):
        def more(i, carry):
            multiply((here + i) % 8, side, False)
            return carry

        lax.fori_loop(1, 8, more, 0)

    for i in (0, 1):
        wait_group(i)
    for h in range(2):
        wait_half(z, x, 1 - c, h)
    multiply(here, 0, True)
    for zz, xx in ((z, left), (z, right), (z, far), (1 - z, x), (1 - z, left), (1 - z, right), (1 - z, far)):
        for h in range(2):
            wait_half(zz, xx, 1 - c, h)
    rest(0)
    send_parts(0)
    for i in (2, 3):
        wait_group(i)
    multiply(here, 1, True)
    rest(1)
    send_parts(1)
    fg_copy.wait_recv()
    fg_ref[...] = fg_all[:, pl.ds(dp * 32, 32)] + fg_in[...]

    for side in range(2):
        view = (slice(None), pl.ds(32 * side, 32))
        for d in range(2):
            wait_bytes(landed.at[(d, *view)], part_recv.at[d, side])
        columns = (landed[0, :, pl.ds(32 * side, 32), :] + landed[1, :, pl.ds(32 * side, 32), :]).reshape(256, 512)
        term = product(columns.T, columns)
        if side == 0:
            gram[...] = term
        else:
            gram[...] += term
    exchanges = []
    for i in range(4):
        view = (pl.ds(128 * i, 128), pl.ds(128 * i, 512 - 128 * i))
        copy = remote(gram.at[view], gram_in.at[view], gram_send.at[i], gram_recv.at[i], dp=1 - dp)
        launch(copy)
        exchanges.append(copy)
    current[...] = (landed[0] + landed[1]).reshape(512, 512).T
    for copy in exchanges:
        copy.wait_recv()
    diagonal = lax.broadcasted_iota(jnp.int32, (128, 128), 0) == lax.broadcasted_iota(jnp.int32, (128, 128), 1)
    trace = jnp.zeros((1, 1), F32)
    for i in range(4):
        block = gram[128 * i : 128 * (i + 1), 128 * i : 128 * (i + 1)]
        block = block + gram_in[128 * i : 128 * (i + 1), 128 * i : 128 * (i + 1)]
        trace = trace + jnp.sum(jnp.where(diagonal, block, 0.0), keepdims=True)
    scale = 1.0 / (jnp.sqrt(trace) + 1e-07)
    for i in range(4):
        for j in range(i, 4):
            at = (slice(128 * i, 128 * (i + 1)), slice(128 * j, 128 * (j + 1)))
            block = (gram[at] + gram_in[at]) * scale * scale
            gram_in[at] = block
            if j > i:
                gram_in[at[1], at[0]] = block.T
    current[...] = current[...] * scale

    def step(i, carry):
        gram_now = gram_in[...]
        mixer = COEF_B * gram_now + COEF_C * product(gram_now, gram_now)
        current[...] = COEF_A * current[...] + product(mixer, current[...])
        half_step = COEF_A * gram_now + product(mixer, gram_now)
        gram_in[...] = COEF_A * half_step + product(half_step, mixer)
        return carry

    lax.fori_loop(0, NS_STEPS - 1, step, 0)
    gram_now = gram_in[...]
    mixer = COEF_B * gram_now + COEF_C * product(gram_now, gram_now)
    update_ref[...] = (COEF_A * current[...] + product(mixer, current[...])) * 32.0

    for side in range(2):
        for j in range(2):
            away, _ = part_copy(j, side)

            @pl.when(jnp.logical_not(stays[j]))
            def _():
                away.wait_send()

    wait_bytes(sent.at[pl.ds(0, 63)], swap_send)
    for copy in pending:
        copy.wait_send()


def gradients(sent, f, tokens):
    tabs = [jnp.asarray(t) for t in fourier_tables()]
    vm = pl.BlockSpec(memory_space=pltpu.VMEM)
    dma = pltpu.SemaphoreType.DMA
    square = pltpu.VMEM((512, 512), F32)
    return pl.pallas_call(
        gradient_kernel,
        out_shape=(
            jax.ShapeDtypeStruct((512, 512), F32),
            jax.ShapeDtypeStruct((64, HALF // 2, RADIX), F32),
        ),
        in_specs=[vm] * 8,
        out_specs=[vm] * 2,
        scratch_shapes=[
            pltpu.VMEM((64, 3, 64, RADIX), BF16),
            pltpu.VMEM((8, 2, 4, RADIX, 1024), BF16),
            pltpu.VMEM((8, GROUPS, HALF, GROUP, RADIX), BF16),
            pltpu.VMEM((2, GROUPS, HALF, GROUP, RADIX), BF16),
            pltpu.VMEM((64, HALF, RADIX), F32),
            pltpu.VMEM((64, HALF // 2, RADIX), F32),
            pltpu.VMEM((3, HALF * GROUP, RADIX), F32),
            pltpu.VMEM((2, HALF * GROUP, RADIX), F32),
            pltpu.VMEM((2, 8, 64, 512), F32),
            pltpu.VMEM((2, 8, 64, 512), F32),
            square, square, square,
            dma, dma, dma, dma((4,)), dma((3,)), dma((8, 2, 2)), dma((32,)), dma((8, GROUPS)), dma((28,)),
            dma((2,)), dma((2, 2)), dma((2, 2)), dma((4,)), dma((4,)),
        ],
        compiler_params=pltpu.CompilerParams(
            collective_id=0, has_side_effects=True, vmem_limit_bytes=60 << 20
        ),
        name="gradients",
    )(sent, f, tokens, *tabs)


def quarters(tokens):
    blocks = tokens.reshape(RADIX, 8, 512)
    return jnp.stack(
        [jnp.concatenate([blocks[:, y], blocks[:, 4 + (y + 2) % 4]], axis=1) for y in range(4)]
    )


def body(tokens, queries, keys, values, upstream, filters):
    conv_grad = (upstream[0].astype(F32) * queries[0].astype(F32)).astype(BF16)
    sent = jnp.stack([item.T.reshape(64, 64, RADIX) for item in (conv_grad, keys[0], values[0])], axis=1)
    f = filters.T.reshape(64, HALF, RADIX)
    update, filter_half = gradients(sent, f, quarters(tokens[0]))
    filter_grad = filter_half.reshape(64, HALF // 2 * RADIX).T
    return (update[None], filter_grad)


def solution(mesh):
    return jax.shard_map(
        body,
        mesh=mesh,
        in_specs=(
            P("dp", "seq", None),
            P("dp", "seq", None),
            P("dp", "seq", None),
            P("dp", "seq", None),
            P("dp", "seq", None),
            P(None, "seq"),
        ),
        out_specs=(P("seq", None, "dp"), P("dp", "seq")),
        check_vma=False,
    )
```

time: 269 us -> 279 us (1.037)
  the two profiles are of different devices: /device:TPU:1 before, /device:TPU:15 now
where the time goes in v3:
time: 279 us
  Pallas kernels  259 us (93%)
  local copies, waits for them, and re-layouts  14.2 us (5%)
  other arithmetic  4.36 us (2%)
    pallas_call x1, Pallas kernels, gradients(): pl.pallas_call(gradient_kernel, out_shape=(jax.ShapeDtypeStruct((512, 512...  259 us
    unnamed x18, local copies, waits for them, and re-layouts  10.2 us

profile of v3, /device:TPU:15, one launch (start us, length us, event | category | flops | bytes accessed | tf_op | source)
XLA Modules:
  0.0 278.7 jit_solution(7909982224742718145)
XLA Ops:
  0.6 1.6 copy.19
  2.3 0.1 fusion.1
  2.3 0.0 copy-start.1
  2.3 0.0 copy-start.2
  2.4 0.1 copy.28
  2.5 0.1 copy.34
  2.6 0.1 copy.33
  2.7 0.1 copy.32
  2.8 0.1 copy.31
  3.0 0.1 copy.30
  3.1 0.8 copy.29
  3.9 1.0 maximum_bitcast_fusion
  4.8 0.1 copy.35
  4.9 0.1 maximum_bitcast_fusion.2
  5.0 1.1 pad_maximum_fusion.1.tok_ref
  6.1 0.0 copy-done.1
  6.1 0.0 copy-done.2
  6.1 0.2 fusion
  6.4 0.7 copy.16
  7.0 1.6 copy.17
  8.7 1.6 copy.18
  10.3 0.0 copy-start
  10.3 2.0 pad_maximum_fusion.sent
  12.3 0.3 copy-done
  12.6 1.7 copy.36
  14.3 259.4 %gradients.1 = (f32[512,512]{1,0:T(8,128)}, f32[64,32,128]{2,1,0:T(8,128)}) custom-call(bf16[64,3,64,128]{3,2,1,0:T(8,128)(2,1)} %pad_maximum_fusion.sent, f32[64,64,128]{2,1,0:T(8,128)} %bitcast.41, bf16[4,128,1024]{2,1,0:T(8,128)(2,1)} %pad_maximum_fusion.1.tok_ref, bf16[144,192]{1,0:T(8,128)(2,1)} %constant.10.clone.t0, ...), custom_call_target="tpu_custom_call" | custom-call | tf_op jit(solution)/shard_map/gradients/pallas_call | solution.py:499
  273.7 2.8 %copy.39 = f32[8,8,32,128]{3,1,2,0:T(8,128)} copy(f32[8,8,32,128]{3,2,1,0:T(8,128)} %bitcast.50) | data formatting | bytes 2097152
  276.5 2.3 copy.41
Async XLA Ops:
  2.3 3.8 %copy-start.1 = (bf16[1,128,4096]{2,1,0:T(8,128)(2,1)S(1)}, bf16[1,128,4096]{2,1,0:T(8,128)(2,1)}, u32[]{:S(2)}) copy-start(bf16[1,128,4096]{2,1,0:T(8,128)(2,1)} %param.12) | copy-start | bytes 3145732
  2.3 3.8 %copy-start.2 = (bf16[1,128,4096]{2,1,0:T(8,128)(2,1)S(1)}, bf16[1,128,4096]{2,1,0:T(8,128)(2,1)}, u32[]{:S(2)}) copy-start(bf16[1,128,4096]{2,1,0:T(8,128)(2,1)} %param.15) | copy-start | bytes 3145732
  10.3 2.3 copy-start

commit v4 on v3

--- a/solution.py
+++ b/solution.py
@@ -147,6 +147,9 @@
     lax.fori_loop(0, GROUP // 2, pair, 0)
 
 
+STRIDE = 37
+
+
 def place():
     me = lax.axis_index("seq")
     return me // 32, me // 8 % 4, me // 2 % 4, me % 2
@@ -182,7 +185,7 @@
     update_ref, fg_ref,
     got, tok, cols, own, fg_all, fg_in, in_rows, out_rows, part, landed, gram, gram_in, current,
     swap_send, swap_recv, swap_own, tok_first, tok_first_send, tok_recv, tok_send, col_recv, col_send,
-    fg_sem, part_send, part_recv, gram_send, gram_recv,
+    fg_sem, part_send, part_recv, gram_send, gram_recv, final_sem,
 ):
     tables = (t0, t1, t2, t3, t4)
     z, x, y, c = place()
@@ -194,9 +197,12 @@
     sibling = seq_of(z, x, y, 1 - c)
     x_right, x_left = seq_of(z, right, y, c), seq_of(z, left, y, c)
     z_other = seq_of(1 - z, x, y, c)
-    targets = [seq_of(j, (y + 2 * j) % 4, 2 * c + z, x // 2) for j in range(2)]
+    mine = (dp + c + x // 2) % 2
+    mate = seq_of(z, x + 1 - 2 * (x % 2), y, c)
+    owner = seq_of(y // 2, 2 * (y % 2) + mine, 2 * c + z, x // 2)
     owner_dp = x % 2
-    source = seq_of(y % 2, 2 * c + dp, (x + 2 * z) % 4, y // 2)
+    source = seq_of(y % 2, 2 * c + dp, 2 * z + x // 2, y // 2)
+    source_dp = (x + y // 2 + c) % 2
 
     barrier = pltpu.get_barrier_semaphore()
 
@@ -206,17 +212,29 @@
 
     lax.fori_loop(1, n_seq, greet, 0)
     pl.semaphore_signal(barrier, inc=1, device_id={"dp": 1 - dp}, device_id_type=MESH)
-    pl.semaphore_signal(barrier, inc=1, device_id={"seq": source, "dp": 1 - dp}, device_id_type=MESH)
-    pl.semaphore_wait(barrier, n_seq + 2 * ((x + dp) % 2))
-
-    def swap(d, carry):
-        peer = (me + d) % n_seq
-        remote(sent.at[peer], got.at[me], swap_send, swap_recv, seq=peer).start()
-        return carry
-
-    lax.fori_loop(1, n_seq, swap, 0)
-    swap_here = pltpu.make_async_copy(sent.at[me], got.at[me], swap_own)
-    swap_here.start()
+
+    @pl.when(source_dp != dp)
+    def _():
+        pl.semaphore_signal(barrier, inc=1, device_id={"seq": source, "dp": 1 - dp}, device_id_type=MESH)
+
+    pl.semaphore_wait(barrier, n_seq + (owner_dp + dp) % 2)
+
+    def swap(part_at):
+        def one(d, carry):
+            peer = (me + STRIDE * d) % n_seq
+            remote(
+                sent.at[peer, part_at], got.at[part_at, me], swap_send.at[part_at], swap_recv.at[part_at], seq=peer
+            ).start()
+            return carry
+
+        lax.fori_loop(1, n_seq, one, 0)
+        pltpu.make_async_copy(sent.at[me, part_at], got.at[part_at, me], swap_own.at[part_at]).start()
+
+    def wait_swap(part_at):
+        wait_bytes(got.at[part_at, pl.ds(0, 63)], swap_recv.at[part_at])
+        wait_bytes(got.at[part_at, 0], swap_own.at[part_at])
+
+    swap(0)
 
     pending = []
 
@@ -225,15 +243,20 @@
         pending.append(copy)
 
     here = z * 4 + x
+
+    def quarter(at):
+        return tok_ref.at[:, pl.ds(pl.multiple_of(at * 1024, 1024), 1024)]
+
     for i, target in enumerate((up, down, across)):
         launch(
             remote(
-                tok_ref.at[target], tok.at[here, c, y], tok_first_send.at[i], tok_first.at[i],
+                quarter(target), tok.at[here, c, y], tok_first_send.at[i], tok_first.at[i],
                 seq=seq_of(z, x, target, c),
             )
         )
-    local_first = pltpu.make_async_copy(tok_ref.at[y], tok.at[here, c, y], tok_first.at[3])
+    local_first = pltpu.make_async_copy(quarter(y), tok.at[here, c, y], tok_first.at[3])
     local_first.start()
+    swap(1)
 
     count = [0]
 
@@ -304,31 +327,31 @@
 
     def compute_group(i):
         for kind in range(3):
-            in_rows[kind] = got[:, kind, GROUP * i : GROUP * (i + 1), :].astype(F32).reshape(HALF * GROUP, RADIX)
+            in_rows[kind] = got[i // 2, :, kind, pl.ds(GROUP * (i % 2), GROUP), :].astype(F32).reshape(HALF * GROUP, RADIX)
         conv_group(i * GROUP, in_rows, f_ref, fg_all, out_rows, tables)
         for kind in range(2):
             own[kind, i] = out_rows[kind].reshape(HALF, GROUP, RADIX).astype(BF16)
 
-    wait_bytes(got.at[pl.ds(0, 63)], swap_recv)
-    swap_here.wait()
+    wait_swap(0)
+    compute_group(0)
+    send_group(0)
     wait_first()
     spread(z)
     for h in range(2):
         send_half(z, x, h, z_other)
         share(z, x, h)
-    compute_group(0)
-    send_group(0)
-    relay(z)
     compute_group(1)
     send_group(1)
+    relay(z)
+    relay_group(0)
+    for xx, h in ((left, 0), (right, 1)):
+        share(z, xx, h)
+    wait_swap(1)
+    compute_group(2)
+    send_group(2)
     for h in range(2):
         wait_half(1 - z, x, c, h)
     spread(1 - z)
-    relay_group(0)
-    for xx, h in ((left, 0), (right, 1)):
-        share(z, xx, h)
-    compute_group(2)
-    send_group(2)
     relay_group(1)
     for h in range(2):
         share(1 - z, x, h)
@@ -384,26 +407,11 @@
 
         lax.fori_loop(0, 4, tile, 0)
 
-    stays = [jnp.logical_and(target == me, owner_dp == dp) for target in targets]
-
-    def part_copy(j, side):
-        view = (slice(None), pl.ds(32 * side, 32))
-        src, dst = part.at[(j, *view)], landed.at[(dp, *view)]
-        arrival = part_recv.at[dp, side]
-        away = remote(src, dst, part_send.at[j, side], arrival, seq=targets[j], dp=owner_dp)
-        return away, pltpu.make_async_copy(src, dst, arrival)
-
-    def send_parts(side):
-        for j in range(2):
-            away, at_home = part_copy(j, side)
-
-            @pl.when(stays[j])
-            def _():
-                at_home.start()
-
-            @pl.when(jnp.logical_not(stays[j]))
-            def _():
-                away.start()
+    def sum_copy(side):
+        return remote(
+            part.at[1 - mine, :, pl.ds(32 * side, 32)], landed.at[:, pl.ds(32 * side, 32)],
+            part_send.at[side], part_recv.at[side], dp=1 - dp,
+        )
 
     def rest(side):
         def more(i, carry):
@@ -421,20 +429,20 @@
         for h in range(2):
             wait_half(zz, xx, 1 - c, h)
     rest(0)
-    send_parts(0)
+    launch(sum_copy(0))
     for i in (2, 3):
         wait_group(i)
     multiply(here, 1, True)
     rest(1)
-    send_parts(1)
+    launch(sum_copy(1))
     fg_copy.wait_recv()
     fg_ref[...] = fg_all[:, pl.ds(dp * 32, 32)] + fg_in[...]
 
     for side in range(2):
-        view = (slice(None), pl.ds(32 * side, 32))
-        for d in range(2):
-            wait_bytes(landed.at[(d, *view)], part_recv.at[d, side])
-        columns = (landed[0, :, pl.ds(32 * side, 32), :] + landed[1, :, pl.ds(32 * side, 32), :]).reshape(256, 512)
+        sum_copy(side).wait_recv()
+        columns = part[mine, :, pl.ds(32 * side, 32), :] + landed[:, pl.ds(32 * side, 32), :]
+        landed[:, pl.ds(32 * side, 32), :] = columns
+        columns = columns.reshape(256, 512)
         term = product(columns.T, columns)
         if side == 0:
             gram[...] = term
@@ -443,10 +451,10 @@
     exchanges = []
     for i in range(4):
         view = (pl.ds(128 * i, 128), pl.ds(128 * i, 512 - 128 * i))
-        copy = remote(gram.at[view], gram_in.at[view], gram_send.at[i], gram_recv.at[i], dp=1 - dp)
+        copy = remote(gram.at[view], gram_in.at[view], gram_send.at[i], gram_recv.at[i], seq=mate)
         launch(copy)
         exchanges.append(copy)
-    current[...] = (landed[0] + landed[1]).reshape(512, 512).T
+    current[...] = landed[...].reshape(512, 512).T
     for copy in exchanges:
         copy.wait_recv()
     diagonal = lax.broadcasted_iota(jnp.int32, (128, 128), 0) == lax.broadcasted_iota(jnp.int32, (128, 128), 1)
@@ -476,17 +484,26 @@
     lax.fori_loop(0, NS_STEPS - 1, step, 0)
     gram_now = gram_in[...]
     mixer = COEF_B * gram_now + COEF_C * product(gram_now, gram_now)
-    update_ref[...] = (COEF_A * current[...] + product(mixer, current[...])) * 32.0
-
-    for side in range(2):
-        for j in range(2):
-            away, _ = part_copy(j, side)
-
-            @pl.when(jnp.logical_not(stays[j]))
-            def _():
-                away.wait_send()
-
-    wait_bytes(sent.at[pl.ds(0, 63)], swap_send)
+    current[...] = (COEF_A * current[...] + product(mixer, current[...])) * 32.0
+    stays = jnp.logical_and(owner == me, owner_dp == dp)
+    away = remote(current, update_ref, final_sem.at[0], final_sem.at[1], seq=owner, dp=owner_dp)
+
+    @pl.when(stays)
+    def _():
+        pltpu.make_async_copy(current, update_ref, final_sem.at[1]).start()
+
+    @pl.when(jnp.logical_not(stays))
+    def _():
+        away.start()
+
+    wait_bytes(update_ref, final_sem.at[1])
+
+    @pl.when(jnp.logical_not(stays))
+    def _():
+        away.wait_send()
+
+    for i in range(2):
+        wait_bytes(got.at[i, pl.ds(0, 63)], swap_send.at[i])
     for copy in pending:
         copy.wait_send()
 
@@ -505,7 +522,7 @@
         in_specs=[vm] * 8,
         out_specs=[vm] * 2,
         scratch_shapes=[
-            pltpu.VMEM((64, 3, 64, RADIX), BF16),
+            pltpu.VMEM((2, 64, 3, 32, RADIX), BF16),
             pltpu.VMEM((8, 2, 4, RADIX, 1024), BF16),
             pltpu.VMEM((8, GROUPS, HALF, GROUP, RADIX), BF16),
             pltpu.VMEM((2, GROUPS, HALF, GROUP, RADIX), BF16),
@@ -514,10 +531,10 @@
             pltpu.VMEM((3, HALF * GROUP, RADIX), F32),
             pltpu.VMEM((2, HALF * GROUP, RADIX), F32),
             pltpu.VMEM((2, 8, 64, 512), F32),
-            pltpu.VMEM((2, 8, 64, 512), F32),
+            pltpu.VMEM((8, 64, 512), F32),
             square, square, square,
-            dma, dma, dma, dma((4,)), dma((3,)), dma((8, 2, 2)), dma((32,)), dma((8, GROUPS)), dma((28,)),
-            dma((2,)), dma((2, 2)), dma((2, 2)), dma((4,)), dma((4,)),
+            dma((2,)), dma((2,)), dma((2,)), dma((4,)), dma((3,)), dma((8, 2, 2)), dma((32,)), dma((8, GROUPS)), dma((28,)),
+            dma((2,)), dma((2,)), dma((2,)), dma((4,)), dma((4,)), dma((2,)),
         ],
         compiler_params=pltpu.CompilerParams(
             collective_id=0, has_side_effects=True, vmem_limit_bytes=60 << 20
@@ -526,18 +543,11 @@
     )(sent, f, tokens, *tabs)
 
 
-def quarters(tokens):
-    blocks = tokens.reshape(RADIX, 8, 512)
-    return jnp.stack(
-        [jnp.concatenate([blocks[:, y], blocks[:, 4 + (y + 2) % 4]], axis=1) for y in range(4)]
-    )
-
-
 def body(tokens, queries, keys, values, upstream, filters):
     conv_grad = (upstream[0].astype(F32) * queries[0].astype(F32)).astype(BF16)
-    sent = jnp.stack([item.T.reshape(64, 64, RADIX) for item in (conv_grad, keys[0], values[0])], axis=1)
+    sent = jnp.stack([item.T.reshape(64, 2, 32, RADIX) for item in (conv_grad, keys[0], values[0])], axis=2)
     f = filters.T.reshape(64, HALF, RADIX)
-    update, filter_half = gradients(sent, f, quarters(tokens[0]))
+    update, filter_half = gradients(sent, f, tokens[0])
     filter_grad = filter_half.reshape(64, HALF // 2 * RADIX).T
     return (update[None], filter_grad)
 

time: 279 us -> 236 us (0.85)
  the two profiles are of different devices: /device:TPU:15 before, /device:TPU:35 now
where the time goes in v4:
time: 236 us
  Pallas kernels  221 us (94%)
  local copies, waits for them, and re-layouts  9.99 us (4%)
  other arithmetic  3.87 us (2%)
    pallas_call x1, Pallas kernels, gradients(): pl.pallas_call(gradient_kernel, out_shape=(jax.ShapeDtypeStruct((512, 512...  221 us
    unnamed x7, local copies, waits for them, and re-layouts  7.05 us

profile of v4, /device:TPU:35, one launch (start us, length us, event | category | flops | bytes accessed | tf_op | source)
XLA Modules:
  0.0 235.6 jit_solution(16454480203955247568)
XLA Ops:
  0.6 0.0 copy-start.1
  0.6 1.9 fusion
  2.5 0.7 copy.13
  3.2 0.0 copy-done.1
  3.2 0.7 copy.14
  3.9 1.6 copy.15
  5.5 0.0 copy-start
  5.5 2.0 pad_maximum_fusion.sent
  7.5 0.3 copy-done
  7.8 1.7 copy.16
  9.5 221.0 %gradients.1 = (f32[512,512]{1,0:T(8,128)}, f32[64,32,128]{2,1,0:T(8,128)}) custom-call(bf16[64,2,3,32,128]{4,3,2,1,0:T(8,128)(2,1)} %pad_maximum_fusion.sent, f32[64,64,128]{2,1,0:T(8,128)} %bitcast.25, bf16[128,4096]{1,0:T(8,128)(2,1)} %bitcast.30, bf16[144,192]{1,0:T(8,128)(2,1)} %constant.10.clone.t0, bf16[768,256]{1,0:T(8,128)(2,1)} %constant.11.clone.t1, ...), custom_call_target="tpu_custom_call" | custom-call | tf_op jit(solution)/shard_map/gradients/pallas_call | solution.py:516
  230.5 2.8 %copy.19 = f32[8,8,32,128]{3,1,2,0:T(8,128)} copy(f32[8,8,32,128]{3,2,1,0:T(8,128)} %bitcast.34) | data formatting | bytes 2097152
  233.3 2.3 copy.21
Async XLA Ops:
  0.6 2.6 %copy-start.1 = (bf16[1,128,4096]{2,1,0:T(8,128)(2,1)S(1)}, bf16[1,128,4096]{2,1,0:T(8,128)(2,1)}, u32[]{:S(2)}) copy-start(bf16[1,128,4096]{2,1,0:T(8,128)(2,1)} %param.13) | copy-start | bytes 3145732
  5.5 2.3 copy-start

commit v5 on v4

--- a/solution.py
+++ b/solution.py
@@ -128,7 +128,7 @@
 GROUPS = 4
 
 
-def conv_group(at, in_rows, f_ref, fg_ref, out_rows, tables):
+def conv_group(at, stage, in_rows, f_ref, fg_ref, out_rows, tables):
     def pair(j, carry):
         chans = [at + 2 * j, at + 2 * j + 1]
         spots = [pl.ds(2 * j + i, HALF, stride=GROUP) for i in range(2)]
@@ -144,7 +144,7 @@
             out_rows[1, spots[i], :] = back * keys[i]
         return carry
 
-    lax.fori_loop(0, GROUP // 2, pair, 0)
+    lax.fori_loop(stage * GROUP // 4, (stage + 1) * GROUP // 4, pair, 0)
 
 
 STRIDE = 37
@@ -157,6 +157,10 @@
 
 def seq_of(z, x, y, c):
     return ((z * 4 + x) * 4 + y) * 2 + c
+
+
+def row_block(y, j):
+    return y // 2, (y // 2 + j) % 2 * 2 + (y + y // 2) % 2
 
 
 MESH = pl.DeviceIdType.MESH
@@ -197,12 +201,20 @@
     sibling = seq_of(z, x, y, 1 - c)
     x_right, x_left = seq_of(z, right, y, c), seq_of(z, left, y, c)
     z_other = seq_of(1 - z, x, y, c)
-    mine = (dp + c + x // 2) % 2
-    mate = seq_of(z, x + 1 - 2 * (x % 2), y, c)
-    owner = seq_of(y // 2, 2 * (y % 2) + mine, 2 * c + z, x // 2)
-    owner_dp = x % 2
-    source = seq_of(y % 2, 2 * c + dp, 2 * z + x // 2, y // 2)
-    source_dp = (x + y // 2 + c) % 2
+    mine = (x + y + x // 2) % 2
+    kind = (dp + x + y + y // 2) % 2
+    side_here = (c + dp) % 2
+    finish_x = [x // 2 * 2 + (j + y + x // 2) % 2 for j in range(2)]
+    finish_dp = [(c + finish_x[j] + y + y // 2) % 2 for j in range(2)]
+    finish_seq = [seq_of(z, finish_x[j], y, (x + finish_dp[j]) % 2) for j in range(2)]
+    source_seq = seq_of(z, x // 2 * 2 + side_here, y, kind)
+    owner_z, owner_x = row_block(y, mine)
+    owner = seq_of(owner_z, owner_x, 2 * kind + z, x // 2)
+    owner_dp = side_here
+    maker_y = 2 * z + (x + z) % 2
+    maker_x = 2 * c + (x // 2 + z + maker_y + c) % 2
+    maker_dp = (y // 2 + maker_x + maker_y + z) % 2
+    maker = seq_of(y % 2, maker_x, maker_y, (dp + maker_dp) % 2)
 
     barrier = pltpu.get_barrier_semaphore()
 
@@ -213,11 +225,13 @@
     lax.fori_loop(1, n_seq, greet, 0)
     pl.semaphore_signal(barrier, inc=1, device_id={"dp": 1 - dp}, device_id_type=MESH)
 
-    @pl.when(source_dp != dp)
+    pl.semaphore_signal(barrier, inc=1, device_id={"seq": source_seq, "dp": 1 - dp}, device_id_type=MESH)
+
+    @pl.when(maker_dp != dp)
     def _():
-        pl.semaphore_signal(barrier, inc=1, device_id={"seq": source, "dp": 1 - dp}, device_id_type=MESH)
-
-    pl.semaphore_wait(barrier, n_seq + (owner_dp + dp) % 2)
+        pl.semaphore_signal(barrier, inc=1, device_id={"seq": maker, "dp": 1 - dp}, device_id_type=MESH)
+
+    pl.semaphore_wait(barrier, n_seq + 1 + (owner_dp + dp) % 2)
 
     def swap(part_at):
         def one(d, carry):
@@ -244,18 +258,22 @@
 
     here = z * 4 + x
 
-    def quarter(at):
-        return tok_ref.at[:, pl.ds(pl.multiple_of(at * 1024, 1024), 1024)]
-
-    for i, target in enumerate((up, down, across)):
-        launch(
-            remote(
-                quarter(target), tok.at[here, c, y], tok_first_send.at[i], tok_first.at[i],
-                seq=seq_of(z, x, target, c),
+    def quarter(at, j):
+        block_z, block_x = row_block(at, j)
+        return tok_ref.at[:, pl.ds(pl.multiple_of((block_z * 4 + block_x) * 512, 512), 512)]
+
+    def spot(j):
+        return tok.at[here, c, y, :, pl.ds(512 * j, 512)]
+
+    for j in range(2):
+        for i, target in enumerate((up, down, across)):
+            launch(
+                remote(
+                    quarter(target, j), spot(j), tok_first_send.at[2 * i + j], tok_first.at[i, j],
+                    seq=seq_of(z, x, target, c),
+                )
             )
-        )
-    local_first = pltpu.make_async_copy(quarter(y), tok.at[here, c, y], tok_first.at[3])
-    local_first.start()
+        pltpu.make_async_copy(quarter(y, j), spot(j), tok_first.at[3, j]).start()
     swap(1)
 
     count = [0]
@@ -276,9 +294,9 @@
         wait_bytes(half(zz, xx, cc, h), tok_recv.at[zz * 4 + xx, cc, h])
 
     def wait_first():
-        for i, source_y in ((0, down), (1, up), (2, across)):
-            wait_bytes(tok.at[here, c, source_y], tok_first.at[i])
-        local_first.wait()
+        for i, source_y in ((0, down), (1, up), (2, across), (3, y)):
+            for j in range(2):
+                wait_bytes(tok.at[here, c, source_y, :, pl.ds(512 * j, 512)], tok_first.at[i, j])
 
     def spread(zz):
         for a, b in ((0, 1), (1, 0)):
@@ -325,60 +343,53 @@
             )
             forwarded[0] += 1
 
-    def compute_group(i):
-        for kind in range(3):
-            in_rows[kind] = got[i // 2, :, kind, pl.ds(GROUP * (i % 2), GROUP), :].astype(F32).reshape(HALF * GROUP, RADIX)
-        conv_group(i * GROUP, in_rows, f_ref, fg_all, out_rows, tables)
-        for kind in range(2):
-            own[kind, i] = out_rows[kind].reshape(HALF, GROUP, RADIX).astype(BF16)
+    def compute(i, stage):
+        if stage == 0:
+            for kind in range(3):
+                chunk = got[i // 2, :, kind, pl.ds(GROUP * (i % 2), GROUP), :]
+                in_rows[kind] = chunk.astype(F32).reshape(HALF * GROUP, RADIX)
+        conv_group(i * GROUP, stage, in_rows, f_ref, fg_all, out_rows, tables)
+        if stage == 1:
+            for kind in range(2):
+                own[kind, i] = out_rows[kind].reshape(HALF, GROUP, RADIX).astype(BF16)
+            send_group(i)
 
     wait_swap(0)
-    compute_group(0)
-    send_group(0)
+    compute(0, 0)
     wait_first()
     spread(z)
     for h in range(2):
         send_half(z, x, h, z_other)
         share(z, x, h)
-    compute_group(1)
-    send_group(1)
+    compute(0, 1)
+    compute(1, 0)
     relay(z)
+    compute(1, 1)
+    wait_swap(1)
     relay_group(0)
-    for xx, h in ((left, 0), (right, 1)):
-        share(z, xx, h)
-    wait_swap(1)
-    compute_group(2)
-    send_group(2)
+    compute(2, 0)
     for h in range(2):
         wait_half(1 - z, x, c, h)
     spread(1 - z)
+    for xx, h in ((left, 0), (right, 1)):
+        share(z, xx, h)
+    compute(2, 1)
     relay_group(1)
+    for xx, h in ((left, 1), (right, 0)):
+        wait_half(z, xx, c, h)
+        share(z, xx, h)
     for h in range(2):
         share(1 - z, x, h)
-    compute_group(3)
-    send_group(3)
+    compute(3, 0)
+    for h in range(2):
+        wait_half(z, far, c, h)
+        share(z, far, h)
+    relay(1 - z)
+    compute(3, 1)
     fg_copy = remote(
         fg_all.at[:, pl.ds((1 - dp) * 32, 32)], fg_in, fg_sem.at[0], fg_sem.at[1], dp=1 - dp
     )
     launch(fg_copy)
-    relay(1 - z)
-    relay_group(2)
-    for xx, h in ((left, 1), (right, 0)):
-        wait_half(z, xx, c, h)
-        share(z, xx, h)
-    for h in range(2):
-        wait_half(z, far, c, h)
-        share(z, far, h)
-    for xx, h in ((left, 0), (right, 1)):
-        share(1 - z, xx, h)
-    for xx, h in ((left, 1), (right, 0)):
-        wait_half(1 - z, xx, c, h)
-        share(1 - z, xx, h)
-    relay_group(3)
-    for h in range(2):
-        wait_half(1 - z, far, c, h)
-        share(1 - z, far, h)
-
     def wait_group(i):
         for cc in range(2):
             wait_col(slot(y, cc, i))
@@ -407,41 +418,72 @@
 
         lax.fori_loop(0, 4, tile, 0)
 
-    def sum_copy(side):
-        return remote(
-            part.at[1 - mine, :, pl.ds(32 * side, 32)], landed.at[:, pl.ds(32 * side, 32)],
-            part_send.at[side], part_recv.at[side], dp=1 - dp,
+    stays = [jnp.logical_and(finish_seq[j] == me, finish_dp[j] == dp) for j in range(2)]
+
+    def part_copy(j, side):
+        view = (slice(None), pl.ds(32 * side, 32))
+        src, dst, arrival = part.at[(j, *view)], landed.at[(dp, *view)], part_recv.at[dp, side]
+        return (
+            remote(src, dst, part_send.at[j, side], arrival, seq=finish_seq[j], dp=finish_dp[j]),
+            pltpu.make_async_copy(src, dst, arrival),
         )
 
-    def rest(side):
+    def send_parts(side):
+        for j in range(2):
+            away, at_home = part_copy(j, side)
+
+            @pl.when(stays[j])
+            def _():
+                at_home.start()
+
+            @pl.when(jnp.logical_not(stays[j]))
+            def _():
+                away.start()
+
+    def multiply_all(zz, side, fresh):
+        if fresh:
+            multiply(zz * 4 + x, side, True)
+
         def more(i, carry):
-            multiply((here + i) % 8, side, False)
+            multiply(zz * 4 + (x + i) % 4, side, False)
             return carry
 
-        lax.fori_loop(1, 8, more, 0)
-
-    for i in (0, 1):
-        wait_group(i)
+        lax.fori_loop(1 if fresh else 0, 4, more, 0)
+
+    def wait_tokens(zz):
+        for xx in (x, left, right, far):
+            for h in range(2):
+                wait_half(zz, xx, 1 - c, h)
+
+    relay_group(2)
+    wait_group(0)
+    wait_group(1)
+    wait_tokens(z)
+    for xx, h in ((left, 0), (right, 1)):
+        share(1 - z, xx, h)
+    for xx, h in ((left, 1), (right, 0)):
+        wait_half(1 - z, xx, c, h)
+        share(1 - z, xx, h)
+    relay_group(3)
+    multiply_all(z, 0, True)
     for h in range(2):
-        wait_half(z, x, 1 - c, h)
-    multiply(here, 0, True)
-    for zz, xx in ((z, left), (z, right), (z, far), (1 - z, x), (1 - z, left), (1 - z, right), (1 - z, far)):
-        for h in range(2):
-            wait_half(zz, xx, 1 - c, h)
-    rest(0)
-    launch(sum_copy(0))
-    for i in (2, 3):
-        wait_group(i)
-    multiply(here, 1, True)
-    rest(1)
-    launch(sum_copy(1))
+        wait_half(1 - z, far, c, h)
+        share(1 - z, far, h)
+    wait_tokens(1 - z)
+    multiply_all(1 - z, 0, False)
+    send_parts(0)
+    wait_group(2)
+    wait_group(3)
+    multiply_all(z, 1, True)
+    multiply_all(1 - z, 1, False)
+    send_parts(1)
     fg_copy.wait_recv()
     fg_ref[...] = fg_all[:, pl.ds(dp * 32, 32)] + fg_in[...]
 
     for side in range(2):
-        sum_copy(side).wait_recv()
-        columns = part[mine, :, pl.ds(32 * side, 32), :] + landed[:, pl.ds(32 * side, 32), :]
-        landed[:, pl.ds(32 * side, 32), :] = columns
+        for d in range(2):
+            wait_bytes(landed.at[d, :, pl.ds(32 * side, 32)], part_recv.at[d, side])
+        columns = landed[0, :, pl.ds(32 * side, 32), :] + landed[1, :, pl.ds(32 * side, 32), :]
         columns = columns.reshape(256, 512)
         term = product(columns.T, columns)
         if side == 0:
@@ -451,10 +493,10 @@
     exchanges = []
     for i in range(4):
         view = (pl.ds(128 * i, 128), pl.ds(128 * i, 512 - 128 * i))
-        copy = remote(gram.at[view], gram_in.at[view], gram_send.at[i], gram_recv.at[i], seq=mate)
+        copy = remote(gram.at[view], gram_in.at[view], gram_send.at[i], gram_recv.at[i], seq=sibling)
         launch(copy)
         exchanges.append(copy)
-    current[...] = landed[...].reshape(512, 512).T
+    current[...] = (landed[0] + landed[1]).reshape(512, 512).T
     for copy in exchanges:
         copy.wait_recv()
     diagonal = lax.broadcasted_iota(jnp.int32, (128, 128), 0) == lax.broadcasted_iota(jnp.int32, (128, 128), 1)
@@ -485,22 +527,30 @@
     gram_now = gram_in[...]
     mixer = COEF_B * gram_now + COEF_C * product(gram_now, gram_now)
     current[...] = (COEF_A * current[...] + product(mixer, current[...])) * 32.0
-    stays = jnp.logical_and(owner == me, owner_dp == dp)
+    is_owner = jnp.logical_and(owner == me, owner_dp == dp)
     away = remote(current, update_ref, final_sem.at[0], final_sem.at[1], seq=owner, dp=owner_dp)
 
-    @pl.when(stays)
+    @pl.when(is_owner)
     def _():
         pltpu.make_async_copy(current, update_ref, final_sem.at[1]).start()
 
-    @pl.when(jnp.logical_not(stays))
+    @pl.when(jnp.logical_not(is_owner))
     def _():
         away.start()
 
     wait_bytes(update_ref, final_sem.at[1])
 
-    @pl.when(jnp.logical_not(stays))
+    @pl.when(jnp.logical_not(is_owner))
     def _():
         away.wait_send()
+
+    for side in range(2):
+        for j in range(2):
+            away, _ = part_copy(j, side)
+
+            @pl.when(jnp.logical_not(stays[j]))
+            def _():
+                away.wait_send()
 
     for i in range(2):
         wait_bytes(got.at[i, pl.ds(0, 63)], swap_send.at[i])
@@ -531,10 +581,10 @@
             pltpu.VMEM((3, HALF * GROUP, RADIX), F32),
             pltpu.VMEM((2, HALF * GROUP, RADIX), F32),
             pltpu.VMEM((2, 8, 64, 512), F32),
-            pltpu.VMEM((8, 64, 512), F32),
+            pltpu.VMEM((2, 8, 64, 512), F32),
             square, square, square,
-            dma((2,)), dma((2,)), dma((2,)), dma((4,)), dma((3,)), dma((8, 2, 2)), dma((32,)), dma((8, GROUPS)), dma((28,)),
-            dma((2,)), dma((2,)), dma((2,)), dma((4,)), dma((4,)), dma((2,)),
+            dma((2,)), dma((2,)), dma((2,)), dma((4, 2)), dma((6,)), dma((8, 2, 2)), dma((32,)), dma((8, GROUPS)), dma((28,)),
+            dma((2,)), dma((2, 2)), dma((2, 2)), dma((4,)), dma((4,)), dma((2,)),
         ],
         compiler_params=pltpu.CompilerParams(
             collective_id=0, has_side_effects=True, vmem_limit_bytes=60 << 20

time: 236 us -> 222 us (0.941)
  the two profiles are of different devices: /device:TPU:35 before, /device:TPU:1 now
where the time goes in v5:
time: 222 us
  Pallas kernels  207 us (93%)
  local copies, waits for them, and re-layouts  9.99 us (4%)
  other arithmetic  3.87 us (2%)
    pallas_call x1, Pallas kernels, gradients(): pl.pallas_call(gradient_kernel, out_shape=(jax.ShapeDtypeStruct((512, 512...  207 us
    unnamed x7, local copies, waits for them, and re-layouts  7.05 us

profile of v5, /device:TPU:1, one launch (start us, length us, event | category | flops | bytes accessed | tf_op | source)
XLA Modules:
  0.0 221.7 jit_solution(1936604774071209699)
XLA Ops:
  0.6 0.0 copy-start.1
  0.6 1.9 fusion
  2.5 0.7 copy.13
  3.2 0.0 copy-done.1
  3.2 0.7 copy.14
  3.9 1.6 copy.15
  5.5 0.0 copy-start
  5.5 2.0 pad_maximum_fusion.sent
  7.5 0.3 copy-done
  7.8 1.7 copy.16
  9.5 207.2 %gradients.1 = (f32[512,512]{1,0:T(8,128)}, f32[64,32,128]{2,1,0:T(8,128)}) custom-call(bf16[64,2,3,32,128]{4,3,2,1,0:T(8,128)(2,1)} %pad_maximum_fusion.sent, f32[64,64,128]{2,1,0:T(8,128)} %bitcast.25, bf16[128,4096]{1,0:T(8,128)(2,1)} %bitcast.30, bf16[144,192]{1,0:T(8,128)(2,1)} %constant.10.clone.t0, bf16[768,256]{1,0:T(8,128)(2,1)} %constant.11.clone.t1, ...), custom_call_target="tpu_custom_call" | custom-call | tf_op jit(solution)/shard_map/gradients/pallas_call | solution.py:566
  216.7 2.8 %copy.19 = f32[8,8,32,128]{3,1,2,0:T(8,128)} copy(f32[8,8,32,128]{3,2,1,0:T(8,128)} %bitcast.34) | data formatting | bytes 2097152
  219.5 2.3 %copy.21 = f32[1,512,512]{2,1,0:T(8,128)} copy(f32[1,512,512]{2,1,0:T(8,128)} %bitcast.33) | data formatting | bytes 2097152
Async XLA Ops:
  0.6 2.6 %copy-start.1 = (bf16[1,128,4096]{2,1,0:T(8,128)(2,1)S(1)}, bf16[1,128,4096]{2,1,0:T(8,128)(2,1)}, u32[]{:S(2)}) copy-start(bf16[1,128,4096]{2,1,0:T(8,128)(2,1)} %param.13) | copy-start | bytes 3145732
  5.5 2.3 %copy-start = (f32[8192,64]{0,1:T(8,128)S(1)}, f32[8192,64]{0,1:T(8,128)}, u32[]{:S(2)}) copy-start(f32[8192,64]{0,1:T(8,128)} %param.16) | copy-start | bytes 6291460

commit v6 on v5

--- a/solution.py
+++ b/solution.py
@@ -128,7 +128,7 @@
 GROUPS = 4
 
 
-def conv_group(at, stage, in_rows, f_ref, fg_ref, out_rows, tables):
+def conv_group(at, stage, in_rows, fg_rows, out_rows, tables):
     def pair(j, carry):
         chans = [at + 2 * j, at + 2 * j + 1]
         spots = [pl.ds(2 * j + i, HALF, stride=GROUP) for i in range(2)]
@@ -136,10 +136,10 @@
         values = [in_rows[2, spot, :] for spot in spots]
         inputs = [(a * b).astype(BF16) for a, b in zip(keys, values)]
         grads = [in_rows[0, spot, :].astype(BF16) for spot in spots]
-        out = convolve_pair(grads, inputs, [f_ref[chan] for chan in chans], tables)
+        out = convolve_pair(grads, inputs, [in_rows[3, spot, :] for spot in spots], tables)
         for i in range(2):
             back = out[2 * i].astype(BF16).astype(F32)
-            fg_ref[chans[i]] = out[2 * i + 1]
+            fg_rows[pl.ds(chans[i], HALF, stride=64), :] = out[2 * i + 1]
             out_rows[0, spots[i], :] = back * values[i]
             out_rows[1, spots[i], :] = back * keys[i]
         return carry
@@ -185,9 +185,9 @@
 
 
 def gradient_kernel(
-    sent, f_ref, tok_ref, t0, t1, t2, t3, t4,
+    up_ref, q_ref, k_ref, v_ref, f_ref, tok_ref, t0, t1, t2, t3, t4,
     update_ref, fg_ref,
-    got, tok, cols, own, fg_all, fg_in, in_rows, out_rows, part, landed, gram, gram_in, current,
+    sent, got, tok, cols, own, fg_all, fg_in, in_rows, out_rows, part, landed, gram, gram_in, current,
     swap_send, swap_recv, swap_own, tok_first, tok_first_send, tok_recv, tok_send, col_recv, col_send,
     fg_sem, part_send, part_recv, gram_send, gram_recv, final_sem,
 ):
@@ -233,22 +233,44 @@
 
     pl.semaphore_wait(barrier, n_seq + 1 + (owner_dp + dp) % 2)
 
-    def swap(part_at):
-        def one(d, carry):
-            peer = (me + STRIDE * d) % n_seq
-            remote(
-                sent.at[peer, part_at], got.at[part_at, me], swap_send.at[part_at], swap_recv.at[part_at], seq=peer
-            ).start()
-            return carry
-
-        lax.fori_loop(1, n_seq, one, 0)
-        pltpu.make_async_copy(sent.at[me, part_at], got.at[part_at, me], swap_own.at[part_at]).start()
+    def swap_piece(peer, part_at):
+        return remote(
+            sent.at[peer, part_at], got.at[part_at, me], swap_send.at[part_at], swap_recv.at[part_at], seq=peer
+        )
+
+    def swap_here(part_at):
+        return pltpu.make_async_copy(sent.at[me, part_at], got.at[part_at, me], swap_own.at[part_at])
+
+    def prepare(chip):
+        span = pl.ds(pl.multiple_of(chip * RADIX, RADIX), RADIX)
+        conv_grad = up_ref[:, span].astype(F32) * q_ref[:, span].astype(F32)
+        for kind, item in enumerate((conv_grad, k_ref[:, span].astype(F32), v_ref[:, span].astype(F32))):
+            turned = item.T.astype(BF16)
+            for core in range(2):
+                for part_at in range(2):
+                    at = 64 * core + 32 * part_at
+                    sent[2 * chip + core, part_at, kind] = turned[at : at + 32]
+
+    def first_half(i, carry):
+        chip = (me // 2 + 19 * i) % (n_seq // 2)
+        prepare(chip)
+        for core in range(2):
+            swap_piece(2 * chip + core, 0).start()
+        return carry
+
+    def second_half(d, carry):
+        swap_piece((me + STRIDE * d) % n_seq, 1).start()
+        return carry
 
     def wait_swap(part_at):
         wait_bytes(got.at[part_at, pl.ds(0, 63)], swap_recv.at[part_at])
         wait_bytes(got.at[part_at, 0], swap_own.at[part_at])
 
-    swap(0)
+    prepare(me // 2)
+    swap_piece(sibling, 0).start()
+    for part_at in range(2):
+        swap_here(part_at).start()
+    lax.fori_loop(1, n_seq // 2, first_half, 0)
 
     pending = []
 
@@ -274,7 +296,7 @@
                 )
             )
         pltpu.make_async_copy(quarter(y, j), spot(j), tok_first.at[3, j]).start()
-    swap(1)
+    lax.fori_loop(1, n_seq, second_half, 0)
 
     count = [0]
 
@@ -348,7 +370,11 @@
             for kind in range(3):
                 chunk = got[i // 2, :, kind, pl.ds(GROUP * (i % 2), GROUP), :]
                 in_rows[kind] = chunk.astype(F32).reshape(HALF * GROUP, RADIX)
-        conv_group(i * GROUP, stage, in_rows, f_ref, fg_all, out_rows, tables)
+            for n in range(HALF):
+                in_rows[3, GROUP * n : GROUP * (n + 1), :] = f_ref[
+                    GROUP * i : GROUP * (i + 1), RADIX * n : RADIX * (n + 1)
+                ]
+        conv_group(i * GROUP, stage, in_rows, fg_all, out_rows, tables)
         if stage == 1:
             for kind in range(2):
                 own[kind, i] = out_rows[kind].reshape(HALF, GROUP, RADIX).astype(BF16)
@@ -387,7 +413,7 @@
     relay(1 - z)
     compute(3, 1)
     fg_copy = remote(
-        fg_all.at[:, pl.ds((1 - dp) * 32, 32)], fg_in, fg_sem.at[0], fg_sem.at[1], dp=1 - dp
+        fg_all.at[pl.ds(pl.multiple_of((1 - dp) * 2048, 2048), 2048)], fg_in, fg_sem.at[0], fg_sem.at[1], dp=1 - dp
     )
     launch(fg_copy)
     def wait_group(i):
@@ -478,7 +504,9 @@
     multiply_all(1 - z, 1, False)
     send_parts(1)
     fg_copy.wait_recv()
-    fg_ref[...] = fg_all[:, pl.ds(dp * 32, 32)] + fg_in[...]
+    for n in range(HALF // 2):
+        kept = fg_all[pl.ds(pl.multiple_of(dp * 2048 + 64 * n, 64), 64), :]
+        fg_ref[:, RADIX * n : RADIX * (n + 1)] = kept + fg_in[64 * n : 64 * (n + 1), :]
 
     for side in range(2):
         for d in range(2):
@@ -526,7 +554,7 @@
     lax.fori_loop(0, NS_STEPS - 1, step, 0)
     gram_now = gram_in[...]
     mixer = COEF_B * gram_now + COEF_C * product(gram_now, gram_now)
-    current[...] = (COEF_A * current[...] + product(mixer, current[...])) * 32.0
+    current[...] = COEF_A * current[...] + product(mixer, current[...])
     is_owner = jnp.logical_and(owner == me, owner_dp == dp)
     away = remote(current, update_ref, final_sem.at[0], final_sem.at[1], seq=owner, dp=owner_dp)
 
@@ -558,7 +586,7 @@
         copy.wait_send()
 
 
-def gradients(sent, f, tokens):
+def gradients(upstream, queries, keys, values, f, tokens):
     tabs = [jnp.asarray(t) for t in fourier_tables()]
     vm = pl.BlockSpec(memory_space=pltpu.VMEM)
     dma = pltpu.SemaphoreType.DMA
@@ -567,18 +595,19 @@
         gradient_kernel,
         out_shape=(
             jax.ShapeDtypeStruct((512, 512), F32),
-            jax.ShapeDtypeStruct((64, HALF // 2, RADIX), F32),
+            jax.ShapeDtypeStruct((64, HALF // 2 * RADIX), F32),
         ),
-        in_specs=[vm] * 8,
+        in_specs=[vm] * 11,
         out_specs=[vm] * 2,
         scratch_shapes=[
+            pltpu.VMEM((64, 2, 3, 32, RADIX), BF16),
             pltpu.VMEM((2, 64, 3, 32, RADIX), BF16),
             pltpu.VMEM((8, 2, 4, RADIX, 1024), BF16),
             pltpu.VMEM((8, GROUPS, HALF, GROUP, RADIX), BF16),
             pltpu.VMEM((2, GROUPS, HALF, GROUP, RADIX), BF16),
-            pltpu.VMEM((64, HALF, RADIX), F32),
-            pltpu.VMEM((64, HALF // 2, RADIX), F32),
-            pltpu.VMEM((3, HALF * GROUP, RADIX), F32),
+            pltpu.VMEM((HALF * 64, RADIX), F32),
+            pltpu.VMEM((HALF // 2 * 64, RADIX), F32),
+            pltpu.VMEM((4, HALF * GROUP, RADIX), F32),
             pltpu.VMEM((2, HALF * GROUP, RADIX), F32),
             pltpu.VMEM((2, 8, 64, 512), F32),
             pltpu.VMEM((2, 8, 64, 512), F32),
@@ -590,16 +619,13 @@
             collective_id=0, has_side_effects=True, vmem_limit_bytes=60 << 20
         ),
         name="gradients",
-    )(sent, f, tokens, *tabs)
+    )(upstream, queries, keys, values, f, tokens, *tabs)
 
 
 def body(tokens, queries, keys, values, upstream, filters):
-    conv_grad = (upstream[0].astype(F32) * queries[0].astype(F32)).astype(BF16)
-    sent = jnp.stack([item.T.reshape(64, 2, 32, RADIX) for item in (conv_grad, keys[0], values[0])], axis=2)
-    f = filters.T.reshape(64, HALF, RADIX)
-    update, filter_half = gradients(sent, f, tokens[0])
-    filter_grad = filter_half.reshape(64, HALF // 2 * RADIX).T
-    return (update[None], filter_grad)
+    update, filter_half = gradients(upstream[0], queries[0], keys[0], values[0], filters.T, tokens[0])
+    filter_grad = filter_half.T
+    return (update[None] * 32.0, filter_grad)
 
 
 def solution(mesh):

time: 222 us -> 213 us (0.959)
  local copies, waits for them, and re-layouts: 9.99 us -> 0.97 us
    unnamed x7 -> x3, local copies, waits for them, and re-layouts: 7.05 us -> 0.97 us
    transpose x3 -> x0, local copies, waits for them, and re-layouts: 2.94 us -> none  [body(): item.T.reshape(64, 2, 32, RADIX)]
    mul x0 -> x1, other arithmetic: none -> 2.38 us  [body(): return (update[None] * 32.0, filter_grad)]
where the time goes in v6:
time: 213 us
  Pallas kernels  209 us (98%)
  other arithmetic  2.38 us (1%)
    pallas_call x1, Pallas kernels, gradients(): pl.pallas_call(gradient_kernel, out_shape=(jax.ShapeDtypeStruct((512, 512...  209 us

profile of v6, /device:TPU:1, one launch (start us, length us, event | category | flops | bytes accessed | tf_op | source)
XLA Modules:
  0.0 213.3 jit_solution(13692927661267235726)
XLA Ops:
  0.6 209.3 %gradients.1 = (f32[512,512]{1,0:T(8,128)}, f32[64,4096]{1,0:T(8,128)}) custom-call(bf16[128,4096]{1,0:T(8,128)(2,1)} %bitcast.11, bf16[128,4096]{1,0:T(8,128)(2,1)} %bitcast.12, bf16[128,4096]{1,0:T(8,128)(2,1)} %bitcast.13, bf16[128,4096]{1,0:T(8,128)(2,1)} %bitcast.14, f32[64,8192]{1,0:T(8,128)} %bitcast.9, bf16[128,4096]{1,0:T(8,128)(2,1)} %bitcast.15, ...), custom_call_target="tpu_custom_call" | custom-call | tf_op jit(solution)/shard_map/gradients/pallas_call | solution.py:594
  209.9 0.0 copy-start
  209.9 2.4 %multiply_bitcast_fusion = f32[1,512,512]{2,1,0:T(8,128)} fusion(f32[512,512]{1,0:T(8,128)} %get-tuple-element.4), kind=kLoop, calls=%fused_computation | loop fusion | flops 262144 | bytes 2097152 | tf_op jit(solution)/shard_map/mul | solution.py:628
  212.3 0.0 copy-done
  212.3 1.0 copy.14
Async XLA Ops:
  209.9 2.4 %copy-start = (f32[64,4096]{1,0:T(8,128)S(1)}, f32[64,4096]{1,0:T(8,128)}, u32[]{:S(2)}) copy-start(f32[64,4096]{1,0:T(8,128)} %get-tuple-element.5) | copy-start | bytes 3145732

commit v7 on v6

--- a/solution.py
+++ b/solution.py
@@ -233,13 +233,13 @@
 
     pl.semaphore_wait(barrier, n_seq + 1 + (owner_dp + dp) % 2)
 
-    def swap_piece(peer, part_at):
+    def swap_piece(peer, group_at):
         return remote(
-            sent.at[peer, part_at], got.at[part_at, me], swap_send.at[part_at], swap_recv.at[part_at], seq=peer
+            sent.at[peer, group_at], got.at[group_at, me], swap_send.at[group_at], swap_recv.at[group_at], seq=peer
         )
 
-    def swap_here(part_at):
-        return pltpu.make_async_copy(sent.at[me, part_at], got.at[part_at, me], swap_own.at[part_at])
+    def swap_here(group_at):
+        return pltpu.make_async_copy(sent.at[me, group_at], got.at[group_at, me], swap_own.at[group_at])
 
     def prepare(chip):
         span = pl.ds(pl.multiple_of(chip * RADIX, RADIX), RADIX)
@@ -247,30 +247,33 @@
         for kind, item in enumerate((conv_grad, k_ref[:, span].astype(F32), v_ref[:, span].astype(F32))):
             turned = item.T.astype(BF16)
             for core in range(2):
-                for part_at in range(2):
-                    at = 64 * core + 32 * part_at
-                    sent[2 * chip + core, part_at, kind] = turned[at : at + 32]
-
-    def first_half(i, carry):
+                for i in range(GROUPS):
+                    at = 64 * core + GROUP * i
+                    sent[2 * chip + core, i, kind] = turned[at : at + GROUP]
+
+    def first_group(i, carry):
         chip = (me // 2 + 19 * i) % (n_seq // 2)
         prepare(chip)
         for core in range(2):
             swap_piece(2 * chip + core, 0).start()
         return carry
 
-    def second_half(d, carry):
-        swap_piece((me + STRIDE * d) % n_seq, 1).start()
-        return carry
-
-    def wait_swap(part_at):
-        wait_bytes(got.at[part_at, pl.ds(0, 63)], swap_recv.at[part_at])
-        wait_bytes(got.at[part_at, 0], swap_own.at[part_at])
+    def swap_group(i):
+        def one(d, carry):
+            swap_piece((me + STRIDE * d) % n_seq, i).start()
+            return carry
+
+        lax.fori_loop(1, n_seq, one, 0)
+
+    def wait_swap(group_at):
+        wait_bytes(got.at[group_at, pl.ds(0, 63)], swap_recv.at[group_at])
+        wait_bytes(got.at[group_at, 0], swap_own.at[group_at])
 
     prepare(me // 2)
     swap_piece(sibling, 0).start()
-    for part_at in range(2):
-        swap_here(part_at).start()
-    lax.fori_loop(1, n_seq // 2, first_half, 0)
+    for i in range(GROUPS):
+        swap_here(i).start()
+    lax.fori_loop(1, n_seq // 2, first_group, 0)
 
     pending = []
 
@@ -296,7 +299,7 @@
                 )
             )
         pltpu.make_async_copy(quarter(y, j), spot(j), tok_first.at[3, j]).start()
-    lax.fori_loop(1, n_seq, second_half, 0)
+    swap_group(1)
 
     count = [0]
 
@@ -368,7 +371,7 @@
     def compute(i, stage):
         if stage == 0:
             for kind in range(3):
-                chunk = got[i // 2, :, kind, pl.ds(GROUP * (i % 2), GROUP), :]
+                chunk = got[i, :, kind]
                 in_rows[kind] = chunk.astype(F32).reshape(HALF * GROUP, RADIX)
             for n in range(HALF):
                 in_rows[3, GROUP * n : GROUP * (n + 1), :] = f_ref[
@@ -382,16 +385,19 @@
 
     wait_swap(0)
     compute(0, 0)
+    swap_group(2)
+    swap_group(3)
     wait_first()
     spread(z)
     for h in range(2):
         send_half(z, x, h, z_other)
         share(z, x, h)
     compute(0, 1)
+    wait_swap(1)
     compute(1, 0)
     relay(z)
     compute(1, 1)
-    wait_swap(1)
+    wait_swap(2)
     relay_group(0)
     compute(2, 0)
     for h in range(2):
@@ -406,6 +412,7 @@
         share(z, xx, h)
     for h in range(2):
         share(1 - z, x, h)
+    wait_swap(3)
     compute(3, 0)
     for h in range(2):
         wait_half(z, far, c, h)
@@ -485,13 +492,13 @@
     wait_group(0)
     wait_group(1)
     wait_tokens(z)
+    multiply_all(z, 0, True)
     for xx, h in ((left, 0), (right, 1)):
         share(1 - z, xx, h)
     for xx, h in ((left, 1), (right, 0)):
         wait_half(1 - z, xx, c, h)
         share(1 - z, xx, h)
     relay_group(3)
-    multiply_all(z, 0, True)
     for h in range(2):
         wait_half(1 - z, far, c, h)
         share(1 - z, far, h)
@@ -580,7 +587,7 @@
             def _():
                 away.wait_send()
 
-    for i in range(2):
+    for i in range(GROUPS):
         wait_bytes(got.at[i, pl.ds(0, 63)], swap_send.at[i])
     for copy in pending:
         copy.wait_send()
@@ -600,8 +607,8 @@
         in_specs=[vm] * 11,
         out_specs=[vm] * 2,
         scratch_shapes=[
-            pltpu.VMEM((64, 2, 3, 32, RADIX), BF16),
-            pltpu.VMEM((2, 64, 3, 32, RADIX), BF16),
+            pltpu.VMEM((64, GROUPS, 3, GROUP, RADIX), BF16),
+            pltpu.VMEM((GROUPS, 64, 3, GROUP, RADIX), BF16),
             pltpu.VMEM((8, 2, 4, RADIX, 1024), BF16),
             pltpu.VMEM((8, GROUPS, HALF, GROUP, RADIX), BF16),
             pltpu.VMEM((2, GROUPS, HALF, GROUP, RADIX), BF16),
@@ -612,7 +619,7 @@
             pltpu.VMEM((2, 8, 64, 512), F32),
             pltpu.VMEM((2, 8, 64, 512), F32),
             square, square, square,
-            dma((2,)), dma((2,)), dma((2,)), dma((4, 2)), dma((6,)), dma((8, 2, 2)), dma((32,)), dma((8, GROUPS)), dma((28,)),
+            dma((GROUPS,)), dma((GROUPS,)), dma((GROUPS,)), dma((4, 2)), dma((6,)), dma((8, 2, 2)), dma((32,)), dma((8, GROUPS)), dma((28,)),
             dma((2,)), dma((2, 2)), dma((2, 2)), dma((4,)), dma((4,)), dma((2,)),
         ],
         compiler_params=pltpu.CompilerParams(

time: 213 us -> 209 us (0.981)
  Pallas kernels: 209 us -> 205 us
    pallas_call x1, Pallas kernels: 209 us -> 205 us  [gradients(): pl.pallas_call(gradient_kernel, out_shape=(jax.ShapeDtypeStruct((512, 512...]
where the time goes in v7:
time: 209 us
  Pallas kernels  205 us (98%)
  other arithmetic  2.38 us (1%)
    pallas_call x1, Pallas kernels, gradients(): pl.pallas_call(gradient_kernel, out_shape=(jax.ShapeDtypeStruct((512, 512...  205 us

profile of v7, /device:TPU:1, one launch (start us, length us, event | category | flops | bytes accessed | tf_op | source)
XLA Modules:
  0.0 208.6 jit_solution(9180033718674617765)
XLA Ops:
  0.6 204.6 %gradients.1 = (f32[512,512]{1,0:T(8,128)}, f32[64,4096]{1,0:T(8,128)}) custom-call(bf16[128,4096]{1,0:T(8,128)(2,1)} %bitcast.11, bf16[128,4096]{1,0:T(8,128)(2,1)} %bitcast.12, bf16[128,4096]{1,0:T(8,128)(2,1)} %bitcast.13, bf16[128,4096]{1,0:T(8,128)(2,1)} %bitcast.14, f32[64,8192]{1,0:T(8,128)} %bitcast.9, bf16[128,4096]{1,0:T(8,128)(2,1)} %bitcast.15, ...), custom_call_target="tpu_custom_call" | custom-call | tf_op jit(solution)/shard_map/gradients/pallas_call | solution.py:601
  205.2 0.0 copy-start
  205.2 2.4 %multiply_bitcast_fusion = f32[1,512,512]{2,1,0:T(8,128)} fusion(f32[512,512]{1,0:T(8,128)} %get-tuple-element.4), kind=kLoop, calls=%fused_computation | loop fusion | flops 262144 | bytes 2097152 | tf_op jit(solution)/shard_map/mul | solution.py:635
  207.6 0.0 copy-done
  207.6 1.0 copy.14
Async XLA Ops:
  205.2 2.4 %copy-start = (f32[64,4096]{1,0:T(8,128)S(1)}, f32[64,4096]{1,0:T(8,128)}, u32[]{:S(2)}) copy-start(f32[64,4096]{1,0:T(8,128)} %get-tuple-element.5) | copy-start | bytes 3145732

commit v8 on v7

--- a/solution.py
+++ b/solution.py
@@ -502,8 +502,18 @@
     for h in range(2):
         wait_half(1 - z, far, c, h)
         share(1 - z, far, h)
-    wait_tokens(1 - z)
-    multiply_all(1 - z, 0, False)
+    for xx in (x, left, right):
+        for h in range(2):
+            wait_half(1 - z, xx, 1 - c, h)
+
+    def multiply_near(i, carry):
+        multiply((1 - z) * 4 + (x + i + i // 2) % 4, 0, False)
+        return carry
+
+    lax.fori_loop(0, 3, multiply_near, 0)
+    for h in range(2):
+        wait_half(1 - z, far, 1 - c, h)
+    multiply((1 - z) * 4 + far, 0, False)
     send_parts(0)
     wait_group(2)
     wait_group(3)

time: 209 us -> 209 us (level)
  no operation moved by 1% of the time
where the time goes in v8:
time: 209 us
  Pallas kernels  205 us (98%)
  other arithmetic  2.38 us (1%)
    pallas_call x1, Pallas kernels, gradients(): pl.pallas_call(gradient_kernel, out_shape=(jax.ShapeDtypeStruct((512, 512...  205 us

profile of v8, /device:TPU:1, one launch (start us, length us, event | category | flops | bytes accessed | tf_op | source)
XLA Modules:
  0.0 208.6 jit_solution(6429680733987674760)
XLA Ops:
  0.6 204.6 %gradients.1 = (f32[512,512]{1,0:T(8,128)}, f32[64,4096]{1,0:T(8,128)}) custom-call(bf16[128,4096]{1,0:T(8,128)(2,1)} %bitcast.11, bf16[128,4096]{1,0:T(8,128)(2,1)} %bitcast.12, bf16[128,4096]{1,0:T(8,128)(2,1)} %bitcast.13, bf16[128,4096]{1,0:T(8,128)(2,1)} %bitcast.14, f32[64,8192]{1,0:T(8,128)} %bitcast.9, bf16[128,4096]{1,0:T(8,128)(2,1)} %bitcast.15, ...), custom_call_target="tpu_custom_call" | custom-call | tf_op jit(solution)/shard_map/gradients/pallas_call | solution.py:611
  205.2 0.0 copy-start
  205.2 2.4 %multiply_bitcast_fusion = f32[1,512,512]{2,1,0:T(8,128)} fusion(f32[512,512]{1,0:T(8,128)} %get-tuple-element.4), kind=kLoop, calls=%fused_computation | loop fusion | flops 262144 | bytes 2097152 | tf_op jit(solution)/shard_map/mul | solution.py:645
  207.6 0.0 copy-done
  207.6 1.0 copy.14
Async XLA Ops:
  205.2 2.4 %copy-start = (f32[64,4096]{1,0:T(8,128)S(1)}, f32[64,4096]{1,0:T(8,128)}, u32[]{:S(2)}) copy-start(f32[64,4096]{1,0:T(8,128)} %get-tuple-element.5) | copy-start | bytes 3145732
